TPU v7x, 256 devices: a whole 4x4x8 slice. The times are simulated.
256 devices in a mesh: docs: 32 (over x, z), vocab: 8 (over y, core).
Axes of the slice: x: 4, y: 4, z: 8, core: 2. Of those that a mesh axis runs over, the one named last changes fastest.
Arguments:
- tokens: bfloat16 [512, 80, 128], P(('docs', 'vocab')), may hold values from -6 to 6
- token_mask: int32 [512, 80], P(('docs', 'vocab')), may hold values from 0 to 1, as said below
- adapter_weight: bfloat16 [128, 768], replicated, may hold values from -0.5 to 0.5
- norm_gain: float32 [768], replicated, may hold values from 0.1 to 1.9
- head_weight: bfloat16 [768, 30720], P(None, 'vocab'), may hold values from -0.21875 to 0.21875
- head_bias: float32 [30720], P('vocab'), may hold values from -8 to 8
- block_counts: int32 [8, 32], P('vocab'), may hold values from 0 to 2, as said below
Outputs:
- postings: float32 [64, 512, 1024], P('docs', None, 'vocab')
Inputs may be any that keep to these rules, and one draw needn't show every extreme that they name: `token_mask`: each passage's live slots are a prefix of at least 16 slots; the first passage of every run of 16 passages is full. `block_counts`: each row sums to 30, and in each row one owner has exactly 2.
All inputs are finite; a program needn't handle non-finite values.
Results may differ from a plain program's by a relative error of at most 0.0012.
Values may be sent and summed in bfloat16 or wider, within the bound.
A program may use at most 128 MiB of HBM per device.

v0:
```python
import jax
import jax.numpy as jnp
from jax import lax
from jax.sharding import PartitionSpec as P

BLOCK = 128


EPSILON = 1e-05


def layer_norm(adapted, norm_gain):
    row_mean = jnp.mean(adapted, axis=-1, keepdims=True)
    centred = adapted - row_mean
    row_var = jnp.mean(centred * centred, axis=-1, keepdims=True)
    return (centred * lax.rsqrt(row_var + EPSILON) * norm_gain).astype(jnp.bfloat16)


def shards(tokens, token_mask, adapter_weight, norm_gain, head_weight, head_bias, block_counts):
    feature_width = tokens.shape[2]
    group_tokens, group_mask = (
        lax.all_gather(tokens, "vocab", axis=0, tiled=True),
        lax.all_gather(token_mask, "vocab", axis=0, tiled=True),
    )
    adapted = jnp.dot(
        group_tokens.reshape(-1, feature_width), adapter_weight, preferred_element_type=jnp.float32
    )
    hidden = layer_norm(adapted, norm_gain)
    group_size, seq_len = group_mask.shape
    logits = jnp.dot(hidden, head_weight, preferred_element_type=jnp.float32) + head_bias
    impact = jnp.log1p(jnp.maximum(logits, 0.0)).reshape(group_size, seq_len, -1)
    pooled = jnp.max(impact * group_mask.astype(jnp.float32)[:, :, None], axis=1)
    num_blocks = pooled.shape[1] // BLOCK
    term_peak = lax.pmax(jnp.max(pooled, axis=0), "docs")
    pooled = pooled / jnp.maximum(term_peak, 1.0)
    owners = lax.axis_size("docs")
    own_cap = max(2, (num_blocks + owners - 1) // owners + 1)
    counts = block_counts[0]
    starts = jnp.cumsum(counts) - counts
    slot_ids = jnp.arange(own_cap, dtype=jnp.int32)[:, None]
    block_index = jnp.clip(starts[None, :] + slot_ids, 0, num_blocks - 1)
    is_live = (slot_ids < counts[None, :]).astype(jnp.float32)
    blocks = jnp.transpose(pooled.reshape(group_size, num_blocks, BLOCK), (1, 0, 2))
    send_tiles = blocks[block_index] * is_live[:, :, None, None]
    received = lax.all_to_all(send_tiles, "docs", split_axis=1, concat_axis=1, tiled=True)
    postings = received.reshape(own_cap, owners * group_size, BLOCK)
    return postings


def solution(mesh):
    in_specs = (
        P(("docs", "vocab"), None, None),
        P(("docs", "vocab"), None),
        P(),
        P(),
        P(None, "vocab"),
        P("vocab"),
        P("vocab", None),
    )
    out_specs = P("docs", None, "vocab")
    return jax.shard_map(shards, mesh=mesh, in_specs=in_specs, out_specs=out_specs, check_vma=False)
```

profile of v0, /device:TPU:32, one launch (start us, length us, event | category | flops | bytes accessed | tf_op | source)
XLA Modules:
  0.0 222.8 jit_solution(15887845669486488397)
XLA Ops:
  0.0 0.0 copy-start
  0.0 0.0 copy-start.4
  0.0 13.8 %all_gather.6 = bf16[16,80,128]{2,1,0:T(8,128)(2,1)S(1)} all-gather(bf16[2,80,128]{2,1,0:T(8,128)(2,1)} %param.7), channel_id=1, replica_groups=mesh['docs'=32,'vocab'=8] {'vocab'}, dimensions={0}, use_global_device_ids=true | all-gather | bytes 368640 | tf_op jit(solution)/shard_map/all_gather | solution.py:22
  13.8 0.0 copy-done
  13.8 0.7 fusion.5
  14.5 0.0 copy-start.1
  14.5 1.9 copy-done.1
  16.4 0.4 multiply_reduce_fusion.2
  16.9 0.0 copy-done.2
  16.9 10.3 %all-gather = s32[8,2,80]{2,1,0:T(2,128)S(1)} all-gather(s32[1,2,80]{2,1,0:T(2,128)S(1)} %bitcast.29), channel_id=1, replica_groups=mesh['docs'=32,'vocab'=8] {'vocab'}, dimensions={0}, use_global_device_ids=true | all-gather | bytes 5760 | tf_op jit(solution)/shard_map/all_gather | solution.py:23
  27.2 0.1 mul.49
  27.3 0.0 copy-done.5
  27.3 0.0 copy-done.4
  27.3 0.0 copy-start.3
  27.3 21.7 %multiply_reduce_fusion = (f32[3840]{0:T(1024)S(1)}, f32[1280,3840]{1,0:T(8,128)}) fusion(f32[1280]{0:T(1024)S(1)} %mul.49, f32[3840]{0:T(1024)S(1)} %copy-done.4, bf16[768,3840]{1,0:T(8,128)(2,1)} %param.11, f32[1280,768]{0,1:T(8,128)} %copy-done.1, f32[768]{0:T(1024)S(1)} %copy-done.5, f32[1280]{0:T(1024)S(1)} %add_rsqrt_fusion, ...), kind=kOutput, calls=%fused_computation.1 | convolution fusion | flops 7573336064 | bytes 29540352 | tf_op jit(solution)/shard_map/dot_general | solution.py:30
  49.0 140.5 %pmax.7 = f32[3840]{0:T(1024)S(1)} all-reduce(f32[3840]{0:T(1024)S(1)} %get-tuple-element.7), channel_id=1, replica_groups=mesh['docs'=32,'vocab'=8] {'docs'}, use_global_device_ids=true, to_apply=%region_4.0 | all-reduce | flops 3840 | bytes 30720 | tf_op jit(solution)/shard_map/pmax | solution.py:34
  189.5 0.2 reduce-window_clone.1
  189.8 0.1 reshape.115
  189.8 0.1 fusion.4
  189.9 9.2 %multiply_reduce_fusion.1 = f32[16,3840]{1,0:T(8,128)S(1)} fusion(f32[16,80,3840]{2,1,0:T(8,128)} %bitcast.25, f32[16,80]{1,0:T(8,128)S(1)} %bitcast.28), kind=kLoop, calls=%fused_computation.2 | loop fusion | flops 9768960 | bytes 19911680 | tf_op jit(solution)/shard_map/reduce_max | solution.py:32
  199.2 0.6 gather_fusion
  199.8 0.1 copy_multiply_fusion
  200.0 22.0 %all_to_all.5 = f32[2,32,16,128]{3,2,0,1:T(8,128)S(1)} all-to-all(f32[2,32,16,128]{3,2,0,1:T(8,128)S(1)} %copy_multiply_fusion), channel_id=1, replica_groups=mesh['docs'=32,'vocab'=8] {'docs'}, dimensions={1} | all-to-all | bytes 1048576 | tf_op jit(solution)/shard_map/all_to_all | solution.py:45
  222.0 0.8 copy.13
  (11 shorter events, 0.1 us)
Async XLA Ops:
  0.0 13.8 %copy-start = (bf16[128,768]{1,0:T(8,128)(2,1)S(1)}, bf16[128,768]{1,0:T(8,128)(2,1)}, u32[]{:S(2)}) copy-start(bf16[128,768]{1,0:T(8,128)(2,1)} %param.9) | copy-start | bytes 589828
  0.0 16.9 %copy-start.2 = (s32[2,80]{1,0:T(2,128)S(1)}, s32[2,80]{1,0:T(2,128)}, u32[]{:S(2)}) copy-start(s32[2,80]{1,0:T(2,128)} %param.8) | copy-start | bytes 1924
  0.0 27.3 %copy-start.5 = (f32[768]{0:T(1024)S(1)}, f32[768]{0:T(1024)}, u32[]{:S(2)}) copy-start(f32[768]{0:T(1024)} %param.10) | copy-start | bytes 9220
  0.0 27.3 %copy-start.4 = (f32[3840]{0:T(1024)S(1)}, f32[3840]{0:T(1024)}, u32[]{:S(2)}) copy-start(f32[3840]{0:T(1024)} %param.12) | copy-start | bytes 46084
  14.5 1.9 copy-start.1
  27.3 162.2 %copy-start.3 = (s32[1,32]{1,0:T(1,128)S(1)}, s32[1,32]{1,0:T(1,128)}, u32[]{:S(2)}) copy-start(s32[1,32]{1,0:T(1,128)} %param.13) | copy-start | bytes 388
where the time goes:
time: 223 us
  blocking collectives  187 us (84%)
  matrix products  22.4 us (10%)
  other arithmetic  10.2 us (5%)
  local copies, waits for them, and re-layouts  3.55 us (2%)
    pmax x1, blocking collectives, shards(): term_peak = lax.pmax(jnp.max(pooled, axis=0), 'docs')  140 us
    all_to_all x1, blocking collectives, shards(): lax.all_to_all(send_tiles, 'docs', split_axis=1, concat_axis=1, tiled=True)  22 us
    dot_general x1, matrix products, shards(): jnp.dot(hidden, head_weight, preferred_element_type=jnp.float32) + head_bias  21.7 us
    all_gather x1, blocking collectives, shards(): lax.all_gather(tokens, 'vocab', axis=0, tiled=True)  13.8 us
    all_gather x1, blocking collectives, shards(): lax.all_gather(token_mask, 'vocab', axis=0, tiled=True)  10.3 us
    reduce_max x1, other arithmetic, shards(): jnp.max(impact * group_mask.astype(jnp.float32)[:, :, None], axis=1)  9.24 us

commit v1 on v0

v1 whole, which is shorter than its diff:
```python
import functools

import jax
import jax.numpy as jnp
from jax import lax
from jax.experimental import pallas as pl
from jax.experimental.pallas import tpu as pltpu
from jax.sharding import PartitionSpec as P

MESH = pl.DeviceIdType.MESH
BLOCK = 128
EPSILON = 1e-05
OWNERS = 32
CHIPS_Y = 4
NB = 30
LEN = 80
HALF = 8 * LEN
SHARD = 2 * LEN
TILE = 768
STEPS = NB * BLOCK // TILE
PIECE = HALF // STEPS


def index_kernel(
    tok_ref, mask_ref, aw_ref, gain_ref, bias_ref, counts_ref, hw_hbm, recv_ref,
    gtok, hid, wbuf, pooled, send, starts, wsem, tok_send, tok_recv, tile_send, tile_recv, tile_own,
):
    d = lax.axis_index("docs")
    v = lax.axis_index("vocab")
    y = v // 2
    c = v % 2
    y1 = y + 1 - 2 * (y % 2)
    y2 = (y + 2) % CHIPS_Y
    y3 = CHIPS_Y - 1 - y
    pair = y // 2
    near = [y1 * 2 + c, y1 * 2 + 1 - c, y * 2 + 1 - c]
    far = [y3 * 2 + c, y2 * 2 + c, y3 * 2 + 1 - c, y2 * 2 + 1 - c]

    def weight_copy(i):
        cols = pl.ds(pl.multiple_of(i * TILE, BLOCK), TILE)
        return pltpu.make_async_copy(hw_hbm.at[:, cols], wbuf.at[i], wsem.at[i])

    for i in range(STEPS):
        weight_copy(i).start()

    barrier = pltpu.get_barrier_semaphore()
    for partner in near + far:
        pl.semaphore_signal(barrier, inc=1, device_id=(d, partner), device_id_type=MESH)

    def greet(t, carry):
        pl.semaphore_signal(
            barrier, inc=1, device_id=((d + t) % OWNERS, v), device_id_type=MESH
        )
        return carry

    lax.fori_loop(1, OWNERS, greet, 0)

    slot = lax.broadcasted_iota(jnp.int32, (LEN, BLOCK), 0).astype(jnp.float32)
    mine = pl.multiple_of(v * SHARD, 16)
    for p in range(2):
        live = jnp.sum(mask_ref[p : p + 1, :].astype(jnp.float32), axis=1, keepdims=True)
        tok = tok_ref[p].astype(jnp.float32)
        tok = jnp.where(slot < live, tok, tok[0:1, :])
        gtok[pl.ds(pl.multiple_of(mine + p * LEN, 16), LEN), :] = tok.astype(jnp.bfloat16)

    def note_start(o, at):
        starts[o] = jnp.minimum(at, NB - 1)
        return at + counts_ref[0, o]

    lax.fori_loop(0, OWNERS, note_start, jnp.int32(0))

    pl.semaphore_wait(barrier, OWNERS - 1 + 7)

    def token_copy(r, partner, owner):
        rows = pl.ds(pl.multiple_of(owner * SHARD, 16), SHARD)
        return pltpu.make_async_remote_copy(
            src_ref=gtok.at[rows],
            dst_ref=gtok.at[rows],
            send_sem=tok_send.at[r],
            recv_sem=tok_recv.at[r],
            device_id=(d, partner),
            device_id_type=MESH,
        )

    for r, partner in enumerate(near + far):
        token_copy(r, partner, v).start()

    def norm_rows(src, dst):
        adapted = jnp.dot(
            gtok[pl.ds(pl.multiple_of(src, 16), PIECE), :], aw_ref[...], preferred_element_type=jnp.float32
        )
        centred = adapted - jnp.mean(adapted, axis=-1, keepdims=True)
        row_var = jnp.mean(centred * centred, axis=-1, keepdims=True)
        normed = centred * lax.rsqrt(row_var + EPSILON) * gain_ref[...]
        hid[pl.ds(pl.multiple_of(dst, 16), PIECE), :] = normed.astype(jnp.bfloat16)

    def head_step(k, i):
        logits = jnp.dot(hid[k * HALF : (k + 1) * HALF, :], wbuf[i], preferred_element_type=jnp.float32)
        x = jnp.maximum(jnp.max(logits.reshape(8, LEN, TILE), axis=1) + bias_ref[i], 0.0)
        for _ in range(3):
            x = x * (x + 2.0)
        for q in range(TILE // BLOCK):
            pooled[k, i * (TILE // BLOCK) + q] = x[:, q * BLOCK : (q + 1) * BLOCK]

    def tiles_of(k, o):
        at = starts[o]
        two = jnp.concatenate(
            [pooled[k, at], pooled[k, jnp.minimum(at + 1, NB - 1)]], axis=0
        )
        send[k, o] = two.astype(jnp.bfloat16)

    def send_tiles(k, half):
        def one(t, carry):
            o = (d + t) % OWNERS
            tiles_of(k, o)
            pltpu.make_async_remote_copy(
                src_ref=send.at[k, o],
                dst_ref=recv_ref.at[half, d],
                send_sem=tile_send.at[k],
                recv_sem=tile_recv.at[k],
                device_id=(o, v),
                device_id_type=MESH,
            ).start()
            return carry

        lax.fori_loop(1, OWNERS, one, 0)
        tiles_of(k, d)
        pltpu.make_async_copy(send.at[k, d], recv_ref.at[half, d], tile_own.at[k]).start()

    for r, partner in enumerate(near):
        token_copy(r, v, partner).wait_recv()
    for r, partner in enumerate(far):
        token_copy(r + 3, v, partner).wait_recv()
    for i in range(STEPS):
        weight_copy(i).wait()
    first = pair * HALF

    def norm_first(i, carry):
        norm_rows(first + i * PIECE, i * PIECE)
        return carry

    lax.fori_loop(0, STEPS, norm_first, 0)
    second = (1 - pair) * HALF

    def head_first(i, carry):
        head_step(0, i)
        norm_rows(second + i * PIECE, HALF + i * PIECE)
        return carry

    lax.fori_loop(0, STEPS, head_first, 0)
    send_tiles(0, pair)

    def head_second(i, carry):
        head_step(1, i)
        return carry

    lax.fori_loop(0, STEPS, head_second, 0)
    send_tiles(1, 1 - pair)

    for r, partner in enumerate(near + far):
        token_copy(r, partner, v).wait_send()
    for k, half in enumerate((pair, 1 - pair)):
        pltpu.make_async_copy(send.at[k, d], recv_ref.at[half, d], tile_own.at[k]).wait()
        others = send.at[k, 0 : OWNERS - 1]
        pltpu.make_async_copy(others, others, tile_send.at[k]).wait()
        others = recv_ref.at[half, 0 : OWNERS - 1]
        pltpu.make_async_copy(others, others, tile_recv.at[k]).wait()


def scale_kernel(counts_ref, code_ref, out_ref):
    owner = lax.axis_index("docs")
    count = counts_ref[0, owner]
    for s in range(2):
        code = code_ref[:, :, s * 8 : (s + 1) * 8, :].astype(jnp.float32)
        top = jnp.max(code.reshape(-1, 8, BLOCK), axis=0)
        top = jnp.max(top, axis=0, keepdims=True)
        peak = jnp.maximum(jnp.log1p(top) * 0.125, 1.0)
        factor = jnp.where(s < count, 0.125 / peak, 0.0)
        for h in range(2):
            out_ref[s, :, h] = jnp.log1p(code[h]) * factor


def shards(tokens, token_mask, adapter_weight, norm_gain, head_weight, head_bias, block_counts):
    vmem = pl.BlockSpec(memory_space=pltpu.VMEM)
    smem = pl.BlockSpec(memory_space=pltpu.SMEM)
    hbm = pl.BlockSpec(memory_space=pl.ANY)
    codes = pl.pallas_call(
        index_kernel,
        out_shape=jax.ShapeDtypeStruct((2, OWNERS, 16, BLOCK), jnp.bfloat16),
        in_specs=[vmem, vmem, vmem, vmem, vmem, smem, hbm],
        out_specs=hbm,
        scratch_shapes=[
            pltpu.VMEM((2 * HALF, BLOCK), jnp.bfloat16),
            pltpu.VMEM((2 * HALF, 768), jnp.bfloat16),
            pltpu.VMEM((STEPS, 768, TILE), jnp.bfloat16),
            pltpu.VMEM((2, NB, 8, BLOCK), jnp.float32),
            pltpu.VMEM((2, OWNERS, 16, BLOCK), jnp.bfloat16),
            pltpu.SMEM((OWNERS,), jnp.int32),
            pltpu.SemaphoreType.DMA((STEPS,)),
            pltpu.SemaphoreType.DMA((7,)),
            pltpu.SemaphoreType.DMA((7,)),
            pltpu.SemaphoreType.DMA((2,)),
            pltpu.SemaphoreType.DMA((2,)),
            pltpu.SemaphoreType.DMA((2,)),
        ],
        compiler_params=pltpu.CompilerParams(
            collective_id=0, has_side_effects=True, vmem_limit_bytes=48 * 2**20
        ),
        cost_estimate=pl.CostEstimate(
            flops=8_000_000_000, bytes_accessed=7_000_000, transcendentals=0
        ),
        name="index",
    )(
        tokens,
        token_mask,
        adapter_weight,
        norm_gain.reshape(1, -1),
        head_bias.reshape(STEPS, 1, TILE),
        block_counts,
        head_weight,
    )
    scaled = pl.pallas_call(
        scale_kernel,
        out_shape=jax.ShapeDtypeStruct((2, OWNERS, 2, 8, BLOCK), jnp.float32),
        in_specs=[smem, vmem],
        out_specs=vmem,
        compiler_params=pltpu.CompilerParams(vmem_limit_bytes=8 * 2**20),
        cost_estimate=pl.CostEstimate(flops=4_000_000, bytes_accessed=800_000, transcendentals=131072),
        name="scale",
    )(block_counts, codes)
    return scaled.reshape(2, OWNERS * 16, BLOCK)


def solution(mesh):
    in_specs = (
        P(("docs", "vocab"), None, None),
        P(("docs", "vocab"), None),
        P(),
        P(),
        P(None, "vocab"),
        P("vocab"),
        P("vocab", None),
    )
    out_specs = P("docs", None, "vocab")
    return jax.shard_map(shards, mesh=mesh, in_specs=in_specs, out_specs=out_specs, check_vma=False)
```

time: 223 us -> 43.1 us (0.19)
  the two profiles are of different devices: /device:TPU:32 before, /device:TPU:1 now
where the time goes in v1:
time: 43.1 us; the launch traced here: 42.8 us
  Pallas kernels  38.3 us (89%)
  local copies, waits for them, and re-layouts  4.46 us (10%)
    pallas_call x1, Pallas kernels, shards(): pl.pallas_call(index_kernel, out_shape=jax.ShapeDtypeStruct((2, OWNERS, 1...  36.8 us
    unnamed x8, local copies, waits for them, and re-layouts  3.03 us
    pallas_call x1, Pallas kernels, shards(): pl.pallas_call(scale_kernel, out_shape=jax.ShapeDtypeStruct((2, OWNERS, 2...  1.55 us

profile of v1, /device:TPU:1, one launch (start us, length us, event | category | flops | bytes accessed | tf_op | source)
XLA Modules:
  0.0 42.8 jit_solution(178660928639443999)
XLA Ops:
  0.0 0.7 %reshape.9.gain_ref = f32[1,768]{1,0:T(1,128)S(1)} reshape(f32[768]{0:T(1024)} %param.10) | data formatting | bytes 6144 | tf_op jit(solution)/shard_map/reshape | solution.py:217
  0.7 0.7 %reshape.10.bias_ref = f32[5,1,768]{2,1,0:T(1,128)S(1)} reshape(f32[3840]{0:T(1024)} %param.12) | data formatting | bytes 30720 | tf_op jit(solution)/shard_map/reshape | solution.py:218
  1.4 0.0 copy-start
  1.4 0.6 %copy-done = s32[1,32]{1,0:T(1,128)S(1)} copy-done((s32[1,32]{1,0:T(1,128)S(1)}, s32[1,32]{1,0:T(1,128)}, u32[]{:S(2)}) %copy-start) | copy-done | bytes 152
  2.1 0.0 copy-start.1
  2.1 0.9 %copy-done.1 = bf16[128,768]{1,0:T(8,128)(2,1)S(1)} copy-done((bf16[128,768]{1,0:T(8,128)(2,1)S(1)}, bf16[128,768]{1,0:T(8,128)(2,1)}, u32[]{:S(2)}) %copy-start.1) | copy-done | bytes 196632
  3.0 0.0 copy-start.2
  3.0 0.8 %copy-done.2 = bf16[2,80,128]{2,1,0:T(8,128)(2,1)S(1)} copy-done((bf16[2,80,128]{2,1,0:T(8,128)(2,1)S(1)}, bf16[2,80,128]{2,1,0:T(8,128)(2,1)}, u32[]{:S(2)}) %copy-start.2) | copy-done | bytes 40984
  3.8 0.0 copy-start.3
  3.8 0.7 %copy-done.3 = s32[2,80]{1,0:T(2,128)S(1)} copy-done((s32[2,80]{1,0:T(2,128)S(1)}, s32[2,80]{1,0:T(2,128)}, u32[]{:S(2)}) %copy-start.3) | copy-done | bytes 664
  4.5 36.8 %index.1.code_ref = bf16[2,32,16,128]{3,2,1,0:T(8,128)(2,1)S(1)} custom-call(bf16[2,80,128]{2,1,0:T(8,128)(2,1)S(1)} %copy-done.2, s32[2,80]{1,0:T(2,128)S(1)} %copy-done.3, bf16[128,768]{1,0:T(8,128)(2,1)S(1)} %copy-done.1, f32[1,768]{1,0:T(1,128)S(1)} %reshape.9.gain_ref, f32[5,1,768]{2,1,0:T(1,128)S(1)} %reshape.10.bias_ref, s32[1,32]{1,0:T(1,128)S(1)} %copy-done, ...), custom_call_target="tpu_custom_call" | custom-call | flops 8000000000 | bytes 7000000 | tf_op jit(solution)/shard_map/index/pallas_call | solution.py:187
  41.3 1.5 %scale.1 = f32[2,32,2,8,128]{4,3,2,1,0:T(8,128)} custom-call(s32[1,32]{1,0:T(1,128)S(1)} %copy-done, bf16[2,32,16,128]{3,2,1,0:T(8,128)(2,1)S(1)} %index.1.code_ref), custom_call_target="tpu_custom_call" | custom-call | flops 4000000 | bytes 800000 | tf_op jit(solution)/shard_map/scale/pallas_call | solution.py:222
Async XLA Ops:
  1.4 0.7 %copy-start = (s32[1,32]{1,0:T(1,128)S(1)}, s32[1,32]{1,0:T(1,128)}, u32[]{:S(2)}) copy-start(s32[1,32]{1,0:T(1,128)} %counts_ref.3) | copy-start | bytes 388
  2.1 0.9 %copy-start.1 = (bf16[128,768]{1,0:T(8,128)(2,1)S(1)}, bf16[128,768]{1,0:T(8,128)(2,1)}, u32[]{:S(2)}) copy-start(bf16[128,768]{1,0:T(8,128)(2,1)} %aw_ref.1) | copy-start | bytes 589828
  3.0 0.8 %copy-start.2 = (bf16[2,80,128]{2,1,0:T(8,128)(2,1)S(1)}, bf16[2,80,128]{2,1,0:T(8,128)(2,1)}, u32[]{:S(2)}) copy-start(bf16[2,80,128]{2,1,0:T(8,128)(2,1)} %tok_ref.1) | copy-start | bytes 122884
  3.8 0.7 %copy-start.3 = (s32[2,80]{1,0:T(2,128)S(1)}, s32[2,80]{1,0:T(2,128)}, u32[]{:S(2)}) copy-start(s32[2,80]{1,0:T(2,128)} %mask_ref.1) | copy-start | bytes 1924

commit v2 on v1

--- a/solution.py
+++ b/solution.py
@@ -22,8 +22,10 @@
 
 
 def index_kernel(
-    tok_ref, mask_ref, aw_ref, gain_ref, bias_ref, counts_ref, hw_hbm, recv_ref,
-    gtok, hid, wbuf, pooled, send, starts, wsem, tok_send, tok_recv, tile_send, tile_recv, tile_own,
+    tok_hbm, mask_hbm, aw_hbm, gain_hbm, bias_hbm, counts_hbm, hw_hbm, recv_ref,
+    tok_ref, mask_ref, aw_ref, gain_ref, bias_ref, counts_ref,
+    near_tok, far_tok, hid, wbuf, pooled, send, starts,
+    arg_sem, wsem, tok_send, tok_recv, tile_send, tile_recv, tile_own,
 ):
     d = lax.axis_index("docs")
     v = lax.axis_index("vocab")
@@ -36,8 +38,18 @@
     near = [y1 * 2 + c, y1 * 2 + 1 - c, y * 2 + 1 - c]
     far = [y3 * 2 + c, y2 * 2 + c, y3 * 2 + 1 - c, y2 * 2 + 1 - c]
 
+    arg_copies = [
+        pltpu.make_async_copy(src, dst, arg_sem.at[i])
+        for i, (src, dst) in enumerate((
+            (tok_hbm, tok_ref), (mask_hbm, mask_ref), (aw_hbm, aw_ref),
+            (gain_hbm, gain_ref), (bias_hbm, bias_ref), (counts_hbm, counts_ref),
+        ))
+    ]
+    for copy in arg_copies:
+        copy.start()
+
     def weight_copy(i):
-        cols = pl.ds(pl.multiple_of(i * TILE, BLOCK), TILE)
+        cols = slice(i * TILE, (i + 1) * TILE)
         return pltpu.make_async_copy(hw_hbm.at[:, cols], wbuf.at[i], wsem.at[i])
 
     for i in range(STEPS):
@@ -56,26 +68,20 @@
     lax.fori_loop(1, OWNERS, greet, 0)
 
     slot = lax.broadcasted_iota(jnp.int32, (LEN, BLOCK), 0).astype(jnp.float32)
-    mine = pl.multiple_of(v * SHARD, 16)
+    arg_copies[0].wait()
+    arg_copies[1].wait()
     for p in range(2):
         live = jnp.sum(mask_ref[p : p + 1, :].astype(jnp.float32), axis=1, keepdims=True)
         tok = tok_ref[p].astype(jnp.float32)
         tok = jnp.where(slot < live, tok, tok[0:1, :])
-        gtok[pl.ds(pl.multiple_of(mine + p * LEN, 16), LEN), :] = tok.astype(jnp.bfloat16)
-
-    def note_start(o, at):
-        starts[o] = jnp.minimum(at, NB - 1)
-        return at + counts_ref[0, o]
-
-    lax.fori_loop(0, OWNERS, note_start, jnp.int32(0))
+        near_tok[v % 4, p * LEN : (p + 1) * LEN, :] = tok.astype(jnp.bfloat16)
 
     pl.semaphore_wait(barrier, OWNERS - 1 + 7)
 
     def token_copy(r, partner, owner):
-        rows = pl.ds(pl.multiple_of(owner * SHARD, 16), SHARD)
         return pltpu.make_async_remote_copy(
-            src_ref=gtok.at[rows],
-            dst_ref=gtok.at[rows],
+            src_ref=near_tok.at[owner % 4],
+            dst_ref=(near_tok if r < 3 else far_tok).at[owner % 4],
             send_sem=tok_send.at[r],
             recv_sem=tok_recv.at[r],
             device_id=(d, partner),
@@ -85,18 +91,27 @@
     for r, partner in enumerate(near + far):
         token_copy(r, partner, v).start()
 
-    def norm_rows(src, dst):
-        adapted = jnp.dot(
-            gtok[pl.ds(pl.multiple_of(src, 16), PIECE), :], aw_ref[...], preferred_element_type=jnp.float32
-        )
+    arg_copies[5].wait()
+
+    def note_start(o, at):
+        starts[o] = jnp.minimum(at, NB - 1)
+        return at + counts_ref[0, o]
+
+    lax.fori_loop(0, OWNERS, note_start, jnp.int32(0))
+    for i in (2, 3, 4):
+        arg_copies[i].wait()
+
+    def norm_rows(tok, dst):
+        adapted = jnp.dot(tok, aw_ref[...], preferred_element_type=jnp.float32)
         centred = adapted - jnp.mean(adapted, axis=-1, keepdims=True)
         row_var = jnp.mean(centred * centred, axis=-1, keepdims=True)
-        normed = centred * lax.rsqrt(row_var + EPSILON) * gain_ref[...]
-        hid[pl.ds(pl.multiple_of(dst, 16), PIECE), :] = normed.astype(jnp.bfloat16)
+        normed = centred * lax.rsqrt(row_var + EPSILON) * gain_ref[...].reshape(1, -1)
+        hid[dst : dst + PIECE, :] = normed.astype(jnp.bfloat16)
 
     def head_step(k, i):
+        bias = bias_ref[pl.ds(i * TILE, TILE)].reshape(1, TILE)
         logits = jnp.dot(hid[k * HALF : (k + 1) * HALF, :], wbuf[i], preferred_element_type=jnp.float32)
-        x = jnp.maximum(jnp.max(logits.reshape(8, LEN, TILE), axis=1) + bias_ref[i], 0.0)
+        x = jnp.maximum(jnp.max(logits.reshape(8, LEN, TILE), axis=1) + bias, 0.0)
         for _ in range(3):
             x = x * (x + 2.0)
         for q in range(TILE // BLOCK):
@@ -129,25 +144,16 @@
 
     for r, partner in enumerate(near):
         token_copy(r, v, partner).wait_recv()
+    tok = near_tok[...].reshape(HALF, BLOCK)
+    for i in range(STEPS):
+        norm_rows(tok[i * PIECE : (i + 1) * PIECE], i * PIECE)
     for r, partner in enumerate(far):
         token_copy(r + 3, v, partner).wait_recv()
+    tok = far_tok[...].reshape(HALF, BLOCK)
     for i in range(STEPS):
         weight_copy(i).wait()
-    first = pair * HALF
-
-    def norm_first(i, carry):
-        norm_rows(first + i * PIECE, i * PIECE)
-        return carry
-
-    lax.fori_loop(0, STEPS, norm_first, 0)
-    second = (1 - pair) * HALF
-
-    def head_first(i, carry):
         head_step(0, i)
-        norm_rows(second + i * PIECE, HALF + i * PIECE)
-        return carry
-
-    lax.fori_loop(0, STEPS, head_first, 0)
+        norm_rows(tok[i * PIECE : (i + 1) * PIECE], HALF + i * PIECE)
     send_tiles(0, pair)
 
     def head_second(i, carry):
@@ -183,19 +189,27 @@
 def shards(tokens, token_mask, adapter_weight, norm_gain, head_weight, head_bias, block_counts):
     vmem = pl.BlockSpec(memory_space=pltpu.VMEM)
     smem = pl.BlockSpec(memory_space=pltpu.SMEM)
-    hbm = pl.BlockSpec(memory_space=pl.ANY)
+    hbm = pl.BlockSpec(memory_space=pltpu.HBM)
     codes = pl.pallas_call(
         index_kernel,
         out_shape=jax.ShapeDtypeStruct((2, OWNERS, 16, BLOCK), jnp.bfloat16),
-        in_specs=[vmem, vmem, vmem, vmem, vmem, smem, hbm],
-        out_specs=hbm,
+        in_specs=[hbm] * 7,
+        out_specs=pl.BlockSpec(memory_space=pl.ANY),
         scratch_shapes=[
-            pltpu.VMEM((2 * HALF, BLOCK), jnp.bfloat16),
+            pltpu.VMEM((2, LEN, BLOCK), jnp.bfloat16),
+            pltpu.VMEM((2, LEN), jnp.int32),
+            pltpu.VMEM((BLOCK, 768), jnp.bfloat16),
+            pltpu.VMEM((768,), jnp.float32),
+            pltpu.VMEM((NB * BLOCK,), jnp.float32),
+            pltpu.SMEM((1, OWNERS), jnp.int32),
+            pltpu.VMEM((4, SHARD, BLOCK), jnp.bfloat16),
+            pltpu.VMEM((4, SHARD, BLOCK), jnp.bfloat16),
             pltpu.VMEM((2 * HALF, 768), jnp.bfloat16),
             pltpu.VMEM((STEPS, 768, TILE), jnp.bfloat16),
             pltpu.VMEM((2, NB, 8, BLOCK), jnp.float32),
             pltpu.VMEM((2, OWNERS, 16, BLOCK), jnp.bfloat16),
             pltpu.SMEM((OWNERS,), jnp.int32),
+            pltpu.SemaphoreType.DMA((6,)),
             pltpu.SemaphoreType.DMA((STEPS,)),
             pltpu.SemaphoreType.DMA((7,)),
             pltpu.SemaphoreType.DMA((7,)),
@@ -210,15 +224,12 @@
             flops=8_000_000_000, bytes_accessed=7_000_000, transcendentals=0
         ),
         name="index",
-    )(
-        tokens,
-        token_mask,
-        adapter_weight,
-        norm_gain.reshape(1, -1),
-        head_bias.reshape(STEPS, 1, TILE),
-        block_counts,
-        head_weight,
-    )
+    )(*(
+        pltpu.with_memory_space_constraint(x, pltpu.HBM)
+        for x in (
+            tokens, token_mask, adapter_weight, norm_gain, head_bias, block_counts, head_weight
+        )
+    ))
     scaled = pl.pallas_call(
         scale_kernel,
         out_shape=jax.ShapeDtypeStruct((2, OWNERS, 2, 8, BLOCK), jnp.float32),

time: 43.1 us -> 36.3 us (0.84)
  local copies, waits for them, and re-layouts: 4.46 us -> 0.01 us
  Pallas kernels: 38.3 us -> 36.2 us
    unnamed x8 -> x2, local copies, waits for them, and re-layouts: 3.03 us -> 0.01 us
    pallas_call x1, Pallas kernels: 36.8 us -> 34.7 us  [shards(): pl.pallas_call(index_kernel, out_shape=jax.ShapeDtypeStruct((2, OWNERS, 1...]
    reshape x2 -> x0, local copies, waits for them, and re-layouts: 1.42 us -> none  [the longest x1 0.73 us: shards(): head_bias.reshape(STEPS, 1, TILE)]
where the time goes in v2:
time: 36.3 us
  Pallas kernels  36.2 us (100%)
    pallas_call x1, Pallas kernels, shards(): pl.pallas_call(index_kernel, out_shape=jax.ShapeDtypeStruct((2, OWNERS, 1...  34.7 us
    pallas_call x1, Pallas kernels, shards(): pl.pallas_call(scale_kernel, out_shape=jax.ShapeDtypeStruct((2, OWNERS, 2...  1.55 us

profile of v2, /device:TPU:1, one launch (start us, length us, event | category | flops | bytes accessed | tf_op | source)
XLA Modules:
  0.0 36.3 jit_solution(17005350087044425481)
XLA Ops:
  0.0 0.0 copy-start
  0.0 34.7 %index.1.code_ref = bf16[2,32,16,128]{3,2,1,0:T(8,128)(2,1)S(1)} custom-call(bf16[2,80,128]{2,1,0:T(8,128)(2,1)} %tok_hbm.1, s32[2,80]{1,0:T(2,128)} %mask_hbm.1, bf16[128,768]{1,0:T(8,128)(2,1)} %aw_hbm.1, f32[768]{0:T(1024)} %gain_hbm.1, f32[3840]{0:T(1024)} %bias_hbm.1, s32[1,32]{1,0:T(1,128)} %counts_ref.1, bf16[768,3840]{1,0:T(8,128)(2,1)} %hw_hbm.1), custom_call_target="tpu_custom_call" | custom-call | flops 8000000000 | bytes 7000000 | tf_op jit(solution)/shard_map/index/pallas_call | solution.py:193
  34.7 0.0 copy-done
  34.7 1.5 %scale.1 = f32[2,32,2,8,128]{4,3,2,1,0:T(8,128)} custom-call(s32[1,32]{1,0:T(1,128)S(1)} %copy-done, bf16[2,32,16,128]{3,2,1,0:T(8,128)(2,1)S(1)} %index.1.code_ref), custom_call_target="tpu_custom_call" | custom-call | flops 4000000 | bytes 800000 | tf_op jit(solution)/shard_map/scale/pallas_call | solution.py:233
Async XLA Ops:
  0.0 34.7 %copy-start = (s32[1,32]{1,0:T(1,128)S(1)}, s32[1,32]{1,0:T(1,128)}, u32[]{:S(2)}) copy-start(s32[1,32]{1,0:T(1,128)} %counts_ref.1) | copy-start | bytes 388

commit v3 on v2

v3 whole, which is shorter than its diff:
```python
import functools

import jax
import jax.numpy as jnp
from jax import lax
from jax.experimental import pallas as pl
from jax.experimental.pallas import tpu as pltpu
from jax.sharding import PartitionSpec as P

MESH = pl.DeviceIdType.MESH
BLOCK = 128
EPSILON = 1e-05
OWNERS = 32
CHIPS_Y = 4
NB = 30
LEN = 80
SHARD = 2 * LEN
CHUNK = 2 * SHARD
TILE = 768
STEPS = NB * BLOCK // TILE
PIECE = CHUNK // STEPS


def index_kernel(
    tok_hbm, mask_hbm, aw_hbm, gain_hbm, bias_hbm, counts_hbm, hw_hbm, recv_ref,
    tok_ref, mask_ref, aw_ref, gain_ref, bias_ref, counts_ref,
    tok_a, tok_b, tok_c, tok_d, hid, wbuf, pooled, send, starts,
    arg_sem, wsem, tok_send, tok_recv, ready, tile_send, tile_recv, tile_own,
):
    d = lax.axis_index("docs")
    v = lax.axis_index("vocab")
    y = v // 2
    c = v % 2
    y1 = y + 1 - 2 * (y % 2)
    y3 = CHIPS_Y - 1 - y
    sibling, near, far = y * 2 + 1 - c, y1 * 2 + c, y3 * 2 + c
    flips = [d + 2**b - 2 ** (b + 1) * ((d // 2**b) % 2) for b in range(5)]

    arg_copies = [
        pltpu.make_async_copy(src, dst, arg_sem.at[i])
        for i, (src, dst) in enumerate((
            (tok_hbm, tok_ref), (mask_hbm, mask_ref), (aw_hbm, aw_ref),
            (gain_hbm, gain_ref), (bias_hbm, bias_ref), (counts_hbm, counts_ref),
        ))
    ]
    for copy in arg_copies:
        copy.start()

    def weight_copy(i):
        cols = slice(i * TILE, (i + 1) * TILE)
        return pltpu.make_async_copy(hw_hbm.at[:, cols], wbuf.at[i], wsem.at[i])

    barrier = pltpu.get_barrier_semaphore()
    for partner in (sibling, near, far):
        pl.semaphore_signal(barrier, inc=1, device_id=(d, partner), device_id_type=MESH)
    for partner in flips:
        pl.semaphore_signal(barrier, inc=1, device_id=(partner, v), device_id_type=MESH)
    for i in range(STEPS):
        weight_copy(i).start()

    slot = lax.broadcasted_iota(jnp.int32, (LEN, BLOCK), 0).astype(jnp.float32)
    arg_copies[0].wait()
    arg_copies[1].wait()
    for p in range(2):
        live = jnp.sum(mask_ref[p : p + 1, :].astype(jnp.float32), axis=1, keepdims=True)
        tok = tok_ref[p].astype(jnp.float32)
        tok = jnp.where(slot < live, tok, tok[0:1, :])
        tok_a[c, p * LEN : (p + 1) * LEN, :] = tok.astype(jnp.bfloat16)

    pl.semaphore_wait(barrier, 8)

    def token_copy(r, src, dst, partner, core):
        return pltpu.make_async_remote_copy(
            src_ref=src.at[core],
            dst_ref=dst.at[core],
            send_sem=tok_send.at[r],
            recv_sem=tok_recv.at[r],
            device_id=(d, partner),
            device_id_type=MESH,
        )

    own_sibling = token_copy(0, tok_a, tok_a, sibling, c)
    own_near = token_copy(1, tok_a, tok_b, near, c)
    own_far = token_copy(2, tok_a, tok_c, far, c)
    near_sibling = token_copy(3, tok_b, tok_b, sibling, c)
    near_far = token_copy(4, tok_b, tok_d, far, c)
    far_sibling = token_copy(5, tok_c, tok_c, sibling, c)
    across_sibling = token_copy(6, tok_d, tok_d, sibling, c)
    own_sibling.start()
    own_near.start()
    own_far.start()

    def from_sibling(r, buf):
        token_copy(r, buf, buf, sibling, 1 - c).wait_recv()

    def tell(b):
        pl.semaphore_signal(ready.at[b - 1], inc=1, device_id=(flips[b], v), device_id_type=MESH)

    tell(1)
    arg_copies[5].wait()

    def note_start(o, at):
        starts[o] = jnp.minimum(at, NB - 1)
        return at + counts_ref[0, o]

    lax.fori_loop(0, OWNERS, note_start, jnp.int32(0))
    for i in (2, 3, 4):
        arg_copies[i].wait()

    def norm_rows(tok, chunk, at):
        adapted = jnp.dot(tok, aw_ref[...], preferred_element_type=jnp.float32)
        centred = adapted - jnp.mean(adapted, axis=-1, keepdims=True)
        row_var = jnp.mean(centred * centred, axis=-1, keepdims=True)
        normed = centred * lax.rsqrt(row_var + EPSILON) * gain_ref[...].reshape(1, -1)
        hid[chunk, at : at + tok.shape[0], :] = normed.astype(jnp.bfloat16)

    def head_step(chunk, i):
        bias = bias_ref[i * TILE : (i + 1) * TILE].reshape(1, TILE)
        logits = jnp.dot(hid[chunk], wbuf[i], preferred_element_type=jnp.float32)
        x = jnp.maximum(jnp.max(logits.reshape(4, LEN, TILE), axis=1) + bias, 0.0)
        for _ in range(3):
            x = x * (x + 2.0)
        row = chunk % 2 * 4
        for q in range(TILE // BLOCK):
            pooled[chunk // 2, i * (TILE // BLOCK) + q, row : row + 4] = x[:, q * BLOCK : (q + 1) * BLOCK]

    def tiles_of(k, o):
        at = starts[o]
        two = jnp.concatenate(
            [pooled[k, at], pooled[k, jnp.minimum(at + 1, NB - 1)]], axis=0
        )
        send[k, o] = two.astype(jnp.bfloat16)

    def send_tile(k, t):
        o = (d + t) % OWNERS
        tiles_of(k, o)
        pltpu.make_async_remote_copy(
            src_ref=send.at[k, o],
            dst_ref=recv_ref.at[k, d],
            send_sem=tile_send.at[k],
            recv_sem=tile_recv.at[k],
            device_id=(o, v),
            device_id_type=MESH,
        ).start()

    def keep_tile(k):
        tiles_of(k, d)
        pltpu.make_async_copy(send.at[k, d], recv_ref.at[k, d], tile_own.at[k]).start()

    from_sibling(0, tok_a)
    tok = tok_a[...].reshape(CHUNK, BLOCK)
    for i in range(STEPS):
        norm_rows(tok[i * PIECE : (i + 1) * PIECE], 0, i * PIECE)
    own_near.wait_recv()
    near_sibling.start()
    near_far.start()
    pl.semaphore_wait(ready.at[0], 1)
    tell(2)

    for i in range(STEPS):
        weight_copy(i).wait()
        if i == 1:
            from_sibling(3, tok_b)
            tok = tok_b[...].reshape(CHUNK, BLOCK)
        head_step(0, i)
        if i >= 1:
            rows = CHUNK // (STEPS - 1)
            norm_rows(tok[(i - 1) * rows : i * rows], 1, (i - 1) * rows)
    pl.semaphore_wait(ready.at[1], 1)
    tell(3)
    own_far.wait_recv()
    far_sibling.start()
    token_copy(4, tok_b, tok_d, far, c).wait_recv()
    across_sibling.start()

    for i in range(STEPS):
        if i == 1:
            pl.semaphore_wait(ready.at[2], 1)
            tell(4)
            from_sibling(5, tok_c)
            tok = tok_c[...].reshape(CHUNK, BLOCK)
        head_step(1, i)
        if i >= 1:
            norm_rows(tok[(i - 1) * rows : i * rows], 2, (i - 1) * rows)
    pl.semaphore_wait(ready.at[3], 1)
    from_sibling(6, tok_d)
    tok = tok_d[...].reshape(CHUNK, BLOCK)

    for i in range(STEPS):
        head_step(2, i)
        norm_rows(tok[i * PIECE : (i + 1) * PIECE], 3, i * PIECE)
        for t in range(1 + i, OWNERS, STEPS):
            send_tile(0, t)
    keep_tile(0)
    for i in range(STEPS):
        head_step(3, i)

    def send_second(t, carry):
        send_tile(1, t)
        return carry

    lax.fori_loop(1, OWNERS, send_second, 0)
    keep_tile(1)

    for copy in (own_sibling, own_near, own_far, near_sibling, near_far, far_sibling, across_sibling):
        copy.wait_send()
    for k in range(2):
        pltpu.make_async_copy(send.at[k, d], recv_ref.at[k, d], tile_own.at[k]).wait()
        others = send.at[k, 0 : OWNERS - 1]
        pltpu.make_async_copy(others, others, tile_send.at[k]).wait()
        others = recv_ref.at[k, 0 : OWNERS - 1]
        pltpu.make_async_copy(others, others, tile_recv.at[k]).wait()


def scale_kernel(counts_ref, code_ref, out_ref):
    owner = lax.axis_index("docs")
    y = lax.axis_index("vocab") // 2
    count = counts_ref[0, owner]
    for s in range(2):
        code = code_ref[:, :, s * 8 : (s + 1) * 8, :].astype(jnp.float32)
        top = jnp.max(code.reshape(-1, 8, BLOCK), axis=0)
        top = jnp.max(top, axis=0, keepdims=True)
        peak = jnp.maximum(jnp.log1p(top) * 0.125, 1.0)
        factor = jnp.where(s < count, 0.125 / peak, 0.0)
        for h in range(2):
            rows = jnp.log1p(code[h]) * factor
            swapped = jnp.concatenate([rows[:, 4:], rows[:, :4]], axis=1)
            half = y // 2 if h == 0 else 1 - y // 2
            out_ref[s, :, half] = jnp.where(y % 2 == 1 - h, swapped, rows)


def shards(tokens, token_mask, adapter_weight, norm_gain, head_weight, head_bias, block_counts):
    vmem = pl.BlockSpec(memory_space=pltpu.VMEM)
    smem = pl.BlockSpec(memory_space=pltpu.SMEM)
    hbm = pl.BlockSpec(memory_space=pltpu.HBM)
    codes = pl.pallas_call(
        index_kernel,
        out_shape=jax.ShapeDtypeStruct((2, OWNERS, 16, BLOCK), jnp.bfloat16),
        in_specs=[hbm] * 7,
        out_specs=pl.BlockSpec(memory_space=pl.ANY),
        scratch_shapes=[
            pltpu.VMEM((2, LEN, BLOCK), jnp.bfloat16),
            pltpu.VMEM((2, LEN), jnp.int32),
            pltpu.VMEM((BLOCK, 768), jnp.bfloat16),
            pltpu.VMEM((768,), jnp.float32),
            pltpu.VMEM((NB * BLOCK,), jnp.float32),
            pltpu.SMEM((1, OWNERS), jnp.int32),
            pltpu.VMEM((2, SHARD, BLOCK), jnp.bfloat16),
            pltpu.VMEM((2, SHARD, BLOCK), jnp.bfloat16),
            pltpu.VMEM((2, SHARD, BLOCK), jnp.bfloat16),
            pltpu.VMEM((2, SHARD, BLOCK), jnp.bfloat16),
            pltpu.VMEM((4, CHUNK, 768), jnp.bfloat16),
            pltpu.VMEM((STEPS, 768, TILE), jnp.bfloat16),
            pltpu.VMEM((2, NB, 8, BLOCK), jnp.float32),
            pltpu.VMEM((2, OWNERS, 16, BLOCK), jnp.bfloat16),
            pltpu.SMEM((OWNERS,), jnp.int32),
            pltpu.SemaphoreType.DMA((6,)),
            pltpu.SemaphoreType.DMA((STEPS,)),
            pltpu.SemaphoreType.DMA((7,)),
            pltpu.SemaphoreType.DMA((7,)),
            pltpu.SemaphoreType.REGULAR((4,)),
            pltpu.SemaphoreType.DMA((2,)),
            pltpu.SemaphoreType.DMA((2,)),
            pltpu.SemaphoreType.DMA((2,)),
        ],
        compiler_params=pltpu.CompilerParams(
            collective_id=0, has_side_effects=True, vmem_limit_bytes=48 * 2**20
        ),
        cost_estimate=pl.CostEstimate(
            flops=8_000_000_000, bytes_accessed=7_000_000, transcendentals=0
        ),
        name="index",
    )(*(
        pltpu.with_memory_space_constraint(x, pltpu.HBM)
        for x in (
            tokens, token_mask, adapter_weight, norm_gain, head_bias, block_counts, head_weight
        )
    ))
    scaled = pl.pallas_call(
        scale_kernel,
        out_shape=jax.ShapeDtypeStruct((2, OWNERS, 2, 8, BLOCK), jnp.float32),
        in_specs=[smem, vmem],
        out_specs=vmem,
        compiler_params=pltpu.CompilerParams(vmem_limit_bytes=8 * 2**20),
        cost_estimate=pl.CostEstimate(flops=4_000_000, bytes_accessed=800_000, transcendentals=131072),
        name="scale",
    )(block_counts, codes)
    return scaled.reshape(2, OWNERS * 16, BLOCK)


def solution(mesh):
    in_specs = (
        P(("docs", "vocab"), None, None),
        P(("docs", "vocab"), None),
        P(),
        P(),
        P(None, "vocab"),
        P("vocab"),
        P("vocab", None),
    )
    out_specs = P("docs", None, "vocab")
    return jax.shard_map(shards, mesh=mesh, in_specs=in_specs, out_specs=out_specs, check_vma=False)
```

time: 36.3 us -> 32.6 us (0.90)
  Pallas kernels: 36.2 us -> 32.6 us
    pallas_call x1, Pallas kernels: 34.7 us -> 31 us  [shards(): pl.pallas_call(index_kernel, out_shape=jax.ShapeDtypeStruct((2, OWNERS, 1...]
where the time goes in v3:
time: 32.6 us
  Pallas kernels  32.6 us (100%)
    pallas_call x1, Pallas kernels, shards(): pl.pallas_call(index_kernel, out_shape=jax.ShapeDtypeStruct((2, OWNERS, 1...  31 us
    pallas_call x1, Pallas kernels, shards(): pl.pallas_call(scale_kernel, out_shape=jax.ShapeDtypeStruct((2, OWNERS, 2...  1.59 us

profile of v3, /device:TPU:1, one launch (start us, length us, event | category | flops | bytes accessed | tf_op | source)
XLA Modules:
  0.0 32.6 jit_solution(3967018376349947007)
XLA Ops:
  0.0 0.0 copy-start
  0.0 31.0 %index.1.code_ref = bf16[2,32,16,128]{3,2,1,0:T(8,128)(2,1)S(1)} custom-call(bf16[2,80,128]{2,1,0:T(8,128)(2,1)} %tok_hbm.1, s32[2,80]{1,0:T(2,128)} %mask_hbm.1, bf16[128,768]{1,0:T(8,128)(2,1)} %aw_hbm.1, f32[768]{0:T(1024)} %gain_hbm.1, f32[3840]{0:T(1024)} %bias_hbm.1, s32[1,32]{1,0:T(1,128)} %counts_ref.1, bf16[768,3840]{1,0:T(8,128)(2,1)} %hw_hbm.1), custom_call_target="tpu_custom_call" | custom-call | flops 8000000000 | bytes 7000000 | tf_op jit(solution)/shard_map/index/pallas_call | solution.py:236
  31.0 0.0 copy-done
  31.0 1.6 %scale.1 = f32[2,32,2,8,128]{4,3,2,1,0:T(8,128)} custom-call(s32[1,32]{1,0:T(1,128)S(1)} %copy-done, bf16[2,32,16,128]{3,2,1,0:T(8,128)(2,1)S(1)} %index.1.code_ref), custom_call_target="tpu_custom_call" | custom-call | flops 4000000 | bytes 800000 | tf_op jit(solution)/shard_map/scale/pallas_call | solution.py:279
Async XLA Ops:
  0.0 31.0 %copy-start = (s32[1,32]{1,0:T(1,128)S(1)}, s32[1,32]{1,0:T(1,128)}, u32[]{:S(2)}) copy-start(s32[1,32]{1,0:T(1,128)} %counts_ref.1) | copy-start | bytes 388

commit v4 on v3

--- a/solution.py
+++ b/solution.py
@@ -12,13 +12,14 @@
 EPSILON = 1e-05
 OWNERS = 32
 CHIPS_Y = 4
+SIZE_X = 4
+SIZE_Z = 8
 NB = 30
 LEN = 80
 SHARD = 2 * LEN
 CHUNK = 2 * SHARD
 TILE = 768
 STEPS = NB * BLOCK // TILE
-PIECE = CHUNK // STEPS
 
 
 def index_kernel(
@@ -32,9 +33,15 @@
     y = v // 2
     c = v % 2
     y1 = y + 1 - 2 * (y % 2)
+    y2 = (y + 2) % CHIPS_Y
     y3 = CHIPS_Y - 1 - y
-    sibling, near, far = y * 2 + 1 - c, y1 * 2 + c, y3 * 2 + c
-    flips = [d + 2**b - 2 ** (b + 1) * ((d // 2**b) % 2) for b in range(5)]
+    partners = [y * 2 + 1 - c] + [chip * 2 + core for chip in (y1, y3, y2) for core in (c, 1 - c)]
+    x = d // SIZE_Z
+    z = d % SIZE_Z
+
+    def across(dx, dz):
+        return (x + dx) % SIZE_X * SIZE_Z + (z + dz) % SIZE_Z
+
 
     arg_copies = [
         pltpu.make_async_copy(src, dst, arg_sem.at[i])
@@ -51,10 +58,10 @@
         return pltpu.make_async_copy(hw_hbm.at[:, cols], wbuf.at[i], wsem.at[i])
 
     barrier = pltpu.get_barrier_semaphore()
-    for partner in (sibling, near, far):
+    for partner in partners:
         pl.semaphore_signal(barrier, inc=1, device_id=(d, partner), device_id_type=MESH)
-    for partner in flips:
-        pl.semaphore_signal(barrier, inc=1, device_id=(partner, v), device_id_type=MESH)
+    for dx, dz in ((0, 1), (0, -1), (1, 0), (-1, 0)):
+        pl.semaphore_signal(barrier, inc=1, device_id=(across(dx, dz), v), device_id_type=MESH)
     for i in range(STEPS):
         weight_copy(i).start()
 
@@ -67,36 +74,35 @@
         tok = jnp.where(slot < live, tok, tok[0:1, :])
         tok_a[c, p * LEN : (p + 1) * LEN, :] = tok.astype(jnp.bfloat16)
 
-    pl.semaphore_wait(barrier, 8)
-
-    def token_copy(r, src, dst, partner, core):
+    pl.semaphore_wait(barrier, 11)
+
+    buffers = [tok_a, tok_b, tok_b, tok_c, tok_c, tok_d, tok_d]
+
+    def token_copy(r, core):
         return pltpu.make_async_remote_copy(
-            src_ref=src.at[core],
-            dst_ref=dst.at[core],
+            src_ref=tok_a.at[core],
+            dst_ref=buffers[r].at[core],
             send_sem=tok_send.at[r],
             recv_sem=tok_recv.at[r],
-            device_id=(d, partner),
+            device_id=(d, partners[r]),
             device_id_type=MESH,
         )
 
-    own_sibling = token_copy(0, tok_a, tok_a, sibling, c)
-    own_near = token_copy(1, tok_a, tok_b, near, c)
-    own_far = token_copy(2, tok_a, tok_c, far, c)
-    near_sibling = token_copy(3, tok_b, tok_b, sibling, c)
-    near_far = token_copy(4, tok_b, tok_d, far, c)
-    far_sibling = token_copy(5, tok_c, tok_c, sibling, c)
-    across_sibling = token_copy(6, tok_d, tok_d, sibling, c)
-    own_sibling.start()
-    own_near.start()
-    own_far.start()
-
-    def from_sibling(r, buf):
-        token_copy(r, buf, buf, sibling, 1 - c).wait_recv()
-
-    def tell(b):
-        pl.semaphore_signal(ready.at[b - 1], inc=1, device_id=(flips[b], v), device_id_type=MESH)
-
-    tell(1)
+    def tokens_in(r):
+        token_copy(r, c if r in (1, 3, 5) else 1 - c).wait_recv()
+
+    def tell(r):
+        for way, step in enumerate((1, -1)[: 1 if r == 4 else 2]):
+            to = across(0, step) if r < 3 else across(step, 0)
+            pl.semaphore_signal(ready.at[r, way], inc=1, device_id=(to, v), device_id_type=MESH)
+
+    def told(r):
+        for way in range(1 if r == 4 else 2):
+            pl.semaphore_wait(ready.at[r, way], 1)
+
+    for r in range(5):
+        token_copy(r, c).start()
+    tell(0)
     arg_copies[5].wait()
 
     def note_start(o, at):
@@ -131,8 +137,16 @@
         )
         send[k, o] = two.astype(jnp.bfloat16)
 
+    def hops(t):
+        dx, dz = t
+        return min(dx, SIZE_X - dx) + min(dz, SIZE_Z - dz)
+
+    owners = sorted(
+        ((dx, dz) for dx in range(SIZE_X) for dz in range(SIZE_Z) if dx or dz), key=hops, reverse=True
+    )
+
     def send_tile(k, t):
-        o = (d + t) % OWNERS
+        o = across(*t)
         tiles_of(k, o)
         pltpu.make_async_remote_copy(
             src_ref=send.at[k, o],
@@ -147,63 +161,59 @@
         tiles_of(k, d)
         pltpu.make_async_copy(send.at[k, d], recv_ref.at[k, d], tile_own.at[k]).start()
 
-    from_sibling(0, tok_a)
-    tok = tok_a[...].reshape(CHUNK, BLOCK)
-    for i in range(STEPS):
-        norm_rows(tok[i * PIECE : (i + 1) * PIECE], 0, i * PIECE)
-    own_near.wait_recv()
-    near_sibling.start()
-    near_far.start()
-    pl.semaphore_wait(ready.at[0], 1)
-    tell(2)
-
+    def norm_chunk(chunk, buf, piece, pieces):
+        rows = CHUNK // pieces
+        tok = buf[piece * rows // SHARD, piece * rows % SHARD : piece * rows % SHARD + rows, :]
+        norm_rows(tok, chunk, piece * rows)
+
+    tokens_in(0)
+    for i in range(4):
+        norm_chunk(0, tok_a, i, 4)
+    for r in (5, 6):
+        token_copy(r, c).start()
+    told(0)
+    tell(1)
     for i in range(STEPS):
         weight_copy(i).wait()
+        head_step(0, i)
+        if i == 2:
+            told(1)
+            tell(2)
+
+    told(2)
+    tell(3)
+    tokens_in(1)
+    tokens_in(2)
+    for i in range(4):
+        norm_chunk(1, tok_b, i, 4)
+    tokens_in(3)
+    tokens_in(4)
+    for i in range(STEPS):
+        head_step(1, i)
+        if i < 4:
+            norm_chunk(2, tok_c, i, 4)
         if i == 1:
-            from_sibling(3, tok_b)
-            tok = tok_b[...].reshape(CHUNK, BLOCK)
-        head_step(0, i)
-        if i >= 1:
-            rows = CHUNK // (STEPS - 1)
-            norm_rows(tok[(i - 1) * rows : i * rows], 1, (i - 1) * rows)
-    pl.semaphore_wait(ready.at[1], 1)
-    tell(3)
-    own_far.wait_recv()
-    far_sibling.start()
-    token_copy(4, tok_b, tok_d, far, c).wait_recv()
-    across_sibling.start()
-
-    for i in range(STEPS):
-        if i == 1:
-            pl.semaphore_wait(ready.at[2], 1)
+            told(3)
             tell(4)
-            from_sibling(5, tok_c)
-            tok = tok_c[...].reshape(CHUNK, BLOCK)
-        head_step(1, i)
-        if i >= 1:
-            norm_rows(tok[(i - 1) * rows : i * rows], 2, (i - 1) * rows)
-    pl.semaphore_wait(ready.at[3], 1)
-    from_sibling(6, tok_d)
-    tok = tok_d[...].reshape(CHUNK, BLOCK)
+    told(4)
+    tokens_in(5)
+    tokens_in(6)
 
     for i in range(STEPS):
         head_step(2, i)
-        norm_rows(tok[i * PIECE : (i + 1) * PIECE], 3, i * PIECE)
-        for t in range(1 + i, OWNERS, STEPS):
+        if i < 4:
+            norm_chunk(3, tok_d, i, 4)
+        for t in owners[i * 7 : i * 7 + 7]:
             send_tile(0, t)
     keep_tile(0)
     for i in range(STEPS):
         head_step(3, i)
-
-    def send_second(t, carry):
+    for t in owners:
         send_tile(1, t)
-        return carry
-
-    lax.fori_loop(1, OWNERS, send_second, 0)
     keep_tile(1)
 
-    for copy in (own_sibling, own_near, own_far, near_sibling, near_far, far_sibling, across_sibling):
-        copy.wait_send()
+    for r in range(7):
+        token_copy(r, c).wait_send()
     for k in range(2):
         pltpu.make_async_copy(send.at[k, d], recv_ref.at[k, d], tile_own.at[k]).wait()
         others = send.at[k, 0 : OWNERS - 1]
@@ -258,7 +268,7 @@
             pltpu.SemaphoreType.DMA((STEPS,)),
             pltpu.SemaphoreType.DMA((7,)),
             pltpu.SemaphoreType.DMA((7,)),
-            pltpu.SemaphoreType.REGULAR((4,)),
+            pltpu.SemaphoreType.REGULAR((5, 2)),
             pltpu.SemaphoreType.DMA((2,)),
             pltpu.SemaphoreType.DMA((2,)),
             pltpu.SemaphoreType.DMA((2,)),

time: 32.6 us -> 31.5 us (0.966)
  Pallas kernels: 32.6 us -> 31.4 us
    pallas_call x1, Pallas kernels: 31 us -> 29.8 us  [shards(): pl.pallas_call(index_kernel, out_shape=jax.ShapeDtypeStruct((2, OWNERS, 1...]
where the time goes in v4:
time: 31.5 us; the launch traced here: 31.4 us
  Pallas kernels  31.4 us (100%)
    pallas_call x1, Pallas kernels, shards(): pl.pallas_call(index_kernel, out_shape=jax.ShapeDtypeStruct((2, OWNERS, 1...  29.8 us
    pallas_call x1, Pallas kernels, shards(): pl.pallas_call(scale_kernel, out_shape=jax.ShapeDtypeStruct((2, OWNERS, 2...  1.59 us

profile of v4, /device:TPU:1, one launch (start us, length us, event | category | flops | bytes accessed | tf_op | source)
XLA Modules:
  0.0 31.4 jit_solution(14008436780026590684)
XLA Ops:
  0.0 0.0 copy-start
  0.0 29.8 %index.1.code_ref = bf16[2,32,16,128]{3,2,1,0:T(8,128)(2,1)S(1)} custom-call(bf16[2,80,128]{2,1,0:T(8,128)(2,1)} %tok_hbm.1, s32[2,80]{1,0:T(2,128)} %mask_hbm.1, bf16[128,768]{1,0:T(8,128)(2,1)} %aw_hbm.1, f32[768]{0:T(1024)} %gain_hbm.1, f32[3840]{0:T(1024)} %bias_hbm.1, s32[1,32]{1,0:T(1,128)} %counts_ref.1, bf16[768,3840]{1,0:T(8,128)(2,1)} %hw_hbm.1), custom_call_target="tpu_custom_call" | custom-call | flops 8000000000 | bytes 7000000 | tf_op jit(solution)/shard_map/index/pallas_call | solution.py:246
  29.8 0.0 copy-done
  29.8 1.6 %scale.1 = f32[2,32,2,8,128]{4,3,2,1,0:T(8,128)} custom-call(s32[1,32]{1,0:T(1,128)S(1)} %copy-done, bf16[2,32,16,128]{3,2,1,0:T(8,128)(2,1)S(1)} %index.1.code_ref), custom_call_target="tpu_custom_call" | custom-call | flops 4000000 | bytes 800000 | tf_op jit(solution)/shard_map/scale/pallas_call | solution.py:289
Async XLA Ops:
  0.0 29.8 %copy-start = (s32[1,32]{1,0:T(1,128)S(1)}, s32[1,32]{1,0:T(1,128)}, u32[]{:S(2)}) copy-start(s32[1,32]{1,0:T(1,128)} %counts_ref.1) | copy-start | bytes 388

commit v5 on v4

--- a/solution.py
+++ b/solution.py
@@ -25,7 +25,7 @@
 def index_kernel(
     tok_hbm, mask_hbm, aw_hbm, gain_hbm, bias_hbm, counts_hbm, hw_hbm, recv_ref,
     tok_ref, mask_ref, aw_ref, gain_ref, bias_ref, counts_ref,
-    tok_a, tok_b, tok_c, tok_d, hid, wbuf, pooled, send, starts,
+    tok_own, tok_a, tok_b, tok_c, tok_d, hid, wbuf, pooled, send, starts,
     arg_sem, wsem, tok_send, tok_recv, ready, tile_send, tile_recv, tile_own,
 ):
     d = lax.axis_index("docs")
@@ -72,16 +72,16 @@
         live = jnp.sum(mask_ref[p : p + 1, :].astype(jnp.float32), axis=1, keepdims=True)
         tok = tok_ref[p].astype(jnp.float32)
         tok = jnp.where(slot < live, tok, tok[0:1, :])
-        tok_a[c, p * LEN : (p + 1) * LEN, :] = tok.astype(jnp.bfloat16)
+        tok_own[p * LEN : (p + 1) * LEN, :] = tok.astype(jnp.bfloat16)
 
     pl.semaphore_wait(barrier, 11)
 
-    buffers = [tok_a, tok_b, tok_b, tok_c, tok_c, tok_d, tok_d]
+    buffers = [None, tok_b, tok_b, tok_c, tok_c, tok_d, tok_d]
 
     def token_copy(r, core):
         return pltpu.make_async_remote_copy(
-            src_ref=tok_a.at[core],
-            dst_ref=buffers[r].at[core],
+            src_ref=tok_own,
+            dst_ref=tok_a if r == 0 else buffers[r].at[core],
             send_sem=tok_send.at[r],
             recv_sem=tok_recv.at[r],
             device_id=(d, partners[r]),
@@ -118,7 +118,7 @@
         centred = adapted - jnp.mean(adapted, axis=-1, keepdims=True)
         row_var = jnp.mean(centred * centred, axis=-1, keepdims=True)
         normed = centred * lax.rsqrt(row_var + EPSILON) * gain_ref[...].reshape(1, -1)
-        hid[chunk, at : at + tok.shape[0], :] = normed.astype(jnp.bfloat16)
+        hid[chunk, pl.ds(at, tok.shape[0]), :] = normed.astype(jnp.bfloat16)
 
     def head_step(chunk, i):
         bias = bias_ref[i * TILE : (i + 1) * TILE].reshape(1, TILE)
@@ -166,48 +166,49 @@
         tok = buf[piece * rows // SHARD, piece * rows % SHARD : piece * rows % SHARD + rows, :]
         norm_rows(tok, chunk, piece * rows)
 
+    for i in range(2):
+        norm_rows(tok_own[i * LEN : (i + 1) * LEN], 0, pl.multiple_of(c * SHARD + i * LEN, 16))
     tokens_in(0)
-    for i in range(4):
-        norm_chunk(0, tok_a, i, 4)
     for r in (5, 6):
         token_copy(r, c).start()
+    for i in range(2):
+        norm_rows(tok_a[i * LEN : (i + 1) * LEN], 0, pl.multiple_of((1 - c) * SHARD + i * LEN, 16))
     told(0)
     tell(1)
     for i in range(STEPS):
         weight_copy(i).wait()
+    for i in range(STEPS):
         head_step(0, i)
-        if i == 2:
-            told(1)
-            tell(2)
-
-    told(2)
-    tell(3)
+
     tokens_in(1)
     tokens_in(2)
+    told(1)
+    tell(2)
     for i in range(4):
         norm_chunk(1, tok_b, i, 4)
     tokens_in(3)
     tokens_in(4)
+    told(2)
+    tell(3)
     for i in range(STEPS):
         head_step(1, i)
         if i < 4:
             norm_chunk(2, tok_c, i, 4)
-        if i == 1:
-            told(3)
-            tell(4)
-    told(4)
     tokens_in(5)
     tokens_in(6)
-
+    told(3)
+    tell(4)
     for i in range(STEPS):
         head_step(2, i)
         if i < 4:
             norm_chunk(3, tok_d, i, 4)
-        for t in owners[i * 7 : i * 7 + 7]:
-            send_tile(0, t)
+    told(4)
+
+    for t in owners:
+        send_tile(0, t)
+    for i in range(STEPS):
+        head_step(3, i)
     keep_tile(0)
-    for i in range(STEPS):
-        head_step(3, i)
     for t in owners:
         send_tile(1, t)
     keep_tile(1)
@@ -222,10 +223,11 @@
         pltpu.make_async_copy(others, others, tile_recv.at[k]).wait()
 
 
-def scale_kernel(counts_ref, code_ref, out_ref):
+def scale_kernel(counts_ref, code_ref, out_hbm, out, sem):
     owner = lax.axis_index("docs")
     y = lax.axis_index("vocab") // 2
     count = counts_ref[0, owner]
+    copies = []
     for s in range(2):
         code = code_ref[:, :, s * 8 : (s + 1) * 8, :].astype(jnp.float32)
         top = jnp.max(code.reshape(-1, 8, BLOCK), axis=0)
@@ -235,8 +237,13 @@
         for h in range(2):
             rows = jnp.log1p(code[h]) * factor
             swapped = jnp.concatenate([rows[:, 4:], rows[:, :4]], axis=1)
+            out[s, h] = jnp.where(y % 2 == 1 - h, swapped, rows)
             half = y // 2 if h == 0 else 1 - y // 2
-            out_ref[s, :, half] = jnp.where(y % 2 == 1 - h, swapped, rows)
+            copy = pltpu.make_async_copy(out.at[s, h], out_hbm.at[s, :, half], sem.at[s, h])
+            copy.start()
+            copies.append(copy)
+    for copy in copies:
+        copy.wait()
 
 
 def shards(tokens, token_mask, adapter_weight, norm_gain, head_weight, head_bias, block_counts):
@@ -255,7 +262,8 @@
             pltpu.VMEM((768,), jnp.float32),
             pltpu.VMEM((NB * BLOCK,), jnp.float32),
             pltpu.SMEM((1, OWNERS), jnp.int32),
-            pltpu.VMEM((2, SHARD, BLOCK), jnp.bfloat16),
+            pltpu.VMEM((SHARD, BLOCK), jnp.bfloat16),
+            pltpu.VMEM((SHARD, BLOCK), jnp.bfloat16),
             pltpu.VMEM((2, SHARD, BLOCK), jnp.bfloat16),
             pltpu.VMEM((2, SHARD, BLOCK), jnp.bfloat16),
             pltpu.VMEM((2, SHARD, BLOCK), jnp.bfloat16),
@@ -290,7 +298,11 @@
         scale_kernel,
         out_shape=jax.ShapeDtypeStruct((2, OWNERS, 2, 8, BLOCK), jnp.float32),
         in_specs=[smem, vmem],
-        out_specs=vmem,
+        out_specs=hbm,
+        scratch_shapes=[
+            pltpu.VMEM((2, 2, OWNERS, 8, BLOCK), jnp.float32),
+            pltpu.SemaphoreType.DMA((2, 2)),
+        ],
         compiler_params=pltpu.CompilerParams(vmem_limit_bytes=8 * 2**20),
         cost_estimate=pl.CostEstimate(flops=4_000_000, bytes_accessed=800_000, transcendentals=131072),
         name="scale",

time: 31.5 us -> 30.3 us (0.962)
  Pallas kernels: 31.4 us -> 30.2 us
    pallas_call x1, Pallas kernels: 29.8 us -> 28.7 us  [shards(): pl.pallas_call(index_kernel, out_shape=jax.ShapeDtypeStruct((2, OWNERS, 1...]
where the time goes in v5:
time: 30.3 us; the launch traced here: 30.2 us
  Pallas kernels  30.2 us (100%)
    pallas_call x1, Pallas kernels, shards(): pl.pallas_call(index_kernel, out_shape=jax.ShapeDtypeStruct((2, OWNERS, 1...  28.7 us
    pallas_call x1, Pallas kernels, shards(): pl.pallas_call(scale_kernel, out_shape=jax.ShapeDtypeStruct((2, OWNERS, 2...  1.48 us

profile of v5, /device:TPU:1, one launch (start us, length us, event | category | flops | bytes accessed | tf_op | source)
XLA Modules:
  0.0 30.2 jit_solution(15061280304527996875)
XLA Ops:
  0.0 0.0 copy-start
  0.0 28.7 %index.1.code_ref = bf16[2,32,16,128]{3,2,1,0:T(8,128)(2,1)S(1)} custom-call(bf16[2,80,128]{2,1,0:T(8,128)(2,1)} %tok_hbm.1, s32[2,80]{1,0:T(2,128)} %mask_hbm.1, bf16[128,768]{1,0:T(8,128)(2,1)} %aw_hbm.1, f32[768]{0:T(1024)} %gain_hbm.1, f32[3840]{0:T(1024)} %bias_hbm.1, s32[1,32]{1,0:T(1,128)} %counts_ref.1, bf16[768,3840]{1,0:T(8,128)(2,1)} %hw_hbm.1), custom_call_target="tpu_custom_call" | custom-call | flops 8000000000 | bytes 7000000 | tf_op jit(solution)/shard_map/index/pallas_call | solution.py:253
  28.7 0.0 copy-done
  28.7 1.5 %scale.1 = f32[2,32,2,8,128]{4,3,2,1,0:T(8,128)} custom-call(s32[1,32]{1,0:T(1,128)S(1)} %copy-done, bf16[2,32,16,128]{3,2,1,0:T(8,128)(2,1)S(1)} %index.1.code_ref), custom_call_target="tpu_custom_call" | custom-call | flops 4000000 | bytes 800000 | tf_op jit(solution)/shard_map/scale/pallas_call | solution.py:297
Async XLA Ops:
  0.0 28.7 %copy-start = (s32[1,32]{1,0:T(1,128)S(1)}, s32[1,32]{1,0:T(1,128)}, u32[]{:S(2)}) copy-start(s32[1,32]{1,0:T(1,128)} %counts_ref.1) | copy-start | bytes 388

commit v6 on v5

--- a/solution.py
+++ b/solution.py
@@ -24,9 +24,9 @@
 
 def index_kernel(
     tok_hbm, mask_hbm, aw_hbm, gain_hbm, bias_hbm, counts_hbm, hw_hbm, recv_ref,
-    tok_ref, mask_ref, aw_ref, gain_ref, bias_ref, counts_ref,
-    tok_own, tok_a, tok_b, tok_c, tok_d, hid, wbuf, pooled, send, starts,
-    arg_sem, wsem, tok_send, tok_recv, ready, tile_send, tile_recv, tile_own,
+    tok_ref, mask_ref, aw_ref, gain_ref, bias_ref, bias2, counts_ref,
+    tok_own, tok_a, tok_b, tok_c, tok_d, hid, wbuf, pooled, pooled_last, send, starts, firsts, order_v, order,
+    arg_sem, wsem, order_sem, tok_send, tok_recv, ready, tile_send, tile_recv, tile_own,
 ):
     d = lax.axis_index("docs")
     v = lax.axis_index("vocab")
@@ -53,17 +53,13 @@
     for copy in arg_copies:
         copy.start()
 
-    def weight_copy(i):
-        cols = slice(i * TILE, (i + 1) * TILE)
-        return pltpu.make_async_copy(hw_hbm.at[:, cols], wbuf.at[i], wsem.at[i])
-
     barrier = pltpu.get_barrier_semaphore()
     for partner in partners:
         pl.semaphore_signal(barrier, inc=1, device_id=(d, partner), device_id_type=MESH)
     for dx, dz in ((0, 1), (0, -1), (1, 0), (-1, 0)):
         pl.semaphore_signal(barrier, inc=1, device_id=(across(dx, dz), v), device_id_type=MESH)
-    for i in range(STEPS):
-        weight_copy(i).start()
+    for b in range(NB):
+        pltpu.make_async_copy(hw_hbm.at[:, b * BLOCK : (b + 1) * BLOCK], wbuf.at[b], wsem).start()
 
     slot = lax.broadcasted_iota(jnp.int32, (LEN, BLOCK), 0).astype(jnp.float32)
     arg_copies[0].wait()
@@ -110,8 +106,31 @@
         return at + counts_ref[0, o]
 
     lax.fori_loop(0, OWNERS, note_start, jnp.int32(0))
+
+    def hops(t):
+        dx, dz = t
+        return min(dx, SIZE_X - dx) + min(dz, SIZE_Z - dz)
+
+    owners = sorted(
+        ((dx, dz) for dx in range(SIZE_X) for dz in range(SIZE_Z) if dx or dz), key=hops, reverse=True
+    )
+
+    lane = lax.broadcasted_iota(jnp.int32, (8, BLOCK), 1)
+    block = jnp.zeros((8, BLOCK), jnp.int32)
+    at = jnp.int32(0)
+    for r, t in enumerate(owners + [(0, 0)]):
+        o = across(*t)
+        firsts[r] = jnp.minimum(at, NB - 1)
+        block = jnp.where(lane >= at, starts[o] + lane - at, block)
+        at = at + counts_ref[0, o]
+    order_v[...] = jnp.clip(block, 0, NB - 1)
+    order_copy = pltpu.make_async_copy(order_v, order, order_sem)
+    order_copy.start()
+    pooled_last[...] = jnp.zeros_like(pooled_last)
     for i in (2, 3, 4):
         arg_copies[i].wait()
+    for b in range(NB):
+        bias2[b] = bias_ref[b * BLOCK : (b + 1) * BLOCK].reshape(1, BLOCK)
 
     def norm_rows(tok, chunk, at):
         adapted = jnp.dot(tok, aw_ref[...], preferred_element_type=jnp.float32)
@@ -121,33 +140,38 @@
         hid[chunk, pl.ds(at, tok.shape[0]), :] = normed.astype(jnp.bfloat16)
 
     def head_step(chunk, i):
-        bias = bias_ref[i * TILE : (i + 1) * TILE].reshape(1, TILE)
-        logits = jnp.dot(hid[chunk], wbuf[i], preferred_element_type=jnp.float32)
+        per = TILE // BLOCK
+        at = range(i * per, (i + 1) * per)
+        if chunk == 3:
+            at = [order[0, b] for b in at]
+        bias = jnp.concatenate([bias2[b] for b in at], axis=1)
+        weights = jnp.concatenate([wbuf[b] for b in at], axis=1)
+        logits = jnp.dot(hid[chunk], weights, preferred_element_type=jnp.float32)
         x = jnp.maximum(jnp.max(logits.reshape(4, LEN, TILE), axis=1) + bias, 0.0)
         for _ in range(3):
             x = x * (x + 2.0)
         row = chunk % 2 * 4
-        for q in range(TILE // BLOCK):
-            pooled[chunk // 2, i * (TILE // BLOCK) + q, row : row + 4] = x[:, q * BLOCK : (q + 1) * BLOCK]
-
-    def tiles_of(k, o):
+        for q in range(per):
+            part = x[:, q * BLOCK : (q + 1) * BLOCK]
+            if chunk == 3:
+                pooled_last[i * per + q, row : row + 4] = part
+            else:
+                pooled[chunk // 2, i * per + q, row : row + 4] = part
+
+    row8 = lax.broadcasted_iota(jnp.int32, (8, BLOCK), 0)
+
+    def tiles_of(k, o, r):
         at = starts[o]
-        two = jnp.concatenate(
-            [pooled[k, at], pooled[k, jnp.minimum(at + 1, NB - 1)]], axis=0
-        )
-        send[k, o] = two.astype(jnp.bfloat16)
-
-    def hops(t):
-        dx, dz = t
-        return min(dx, SIZE_X - dx) + min(dz, SIZE_Z - dz)
-
-    owners = sorted(
-        ((dx, dz) for dx in range(SIZE_X) for dz in range(SIZE_Z) if dx or dz), key=hops, reverse=True
-    )
-
-    def send_tile(k, t):
-        o = across(*t)
-        tiles_of(k, o)
+        two = [pooled[k, at], pooled[k, jnp.minimum(at + 1, NB - 1)]]
+        if k == 1:
+            at = firsts[r]
+            late = [pooled_last[at], pooled_last[jnp.minimum(at + 1, NB - 1)]]
+            two = [jnp.where(row8 < 4, a, b) for a, b in zip(two, late)]
+        send[k, o] = jnp.concatenate(two, axis=0).astype(jnp.bfloat16)
+
+    def send_tile(k, r):
+        o = across(*owners[r])
+        tiles_of(k, o, r)
         pltpu.make_async_remote_copy(
             src_ref=send.at[k, o],
             dst_ref=recv_ref.at[k, d],
@@ -158,7 +182,7 @@
         ).start()
 
     def keep_tile(k):
-        tiles_of(k, d)
+        tiles_of(k, d, OWNERS - 1)
         pltpu.make_async_copy(send.at[k, d], recv_ref.at[k, d], tile_own.at[k]).start()
 
     def norm_chunk(chunk, buf, piece, pieces):
@@ -175,15 +199,15 @@
         norm_rows(tok_a[i * LEN : (i + 1) * LEN], 0, pl.multiple_of((1 - c) * SHARD + i * LEN, 16))
     told(0)
     tell(1)
-    for i in range(STEPS):
-        weight_copy(i).wait()
-    for i in range(STEPS):
+    pltpu.make_async_copy(wbuf, wbuf, wsem).wait()
+    for i in range(STEPS - 1):
         head_step(0, i)
 
     tokens_in(1)
     tokens_in(2)
     told(1)
     tell(2)
+    head_step(0, STEPS - 1)
     for i in range(4):
         norm_chunk(1, tok_b, i, 4)
     tokens_in(3)
@@ -204,13 +228,17 @@
             norm_chunk(3, tok_d, i, 4)
     told(4)
 
-    for t in owners:
-        send_tile(0, t)
+    order_copy.wait()
+    for r in range(OWNERS - 1):
+        send_tile(0, r)
+    keep_tile(0)
+    early = TILE // BLOCK // 2
     for i in range(STEPS):
         head_step(3, i)
-    keep_tile(0)
-    for t in owners:
-        send_tile(1, t)
+        for r in range(i * early, min((i + 1) * early, OWNERS - 1)):
+            send_tile(1, r)
+    for r in range(STEPS * early, OWNERS - 1):
+        send_tile(1, r)
     keep_tile(1)
 
     for r in range(7):
@@ -233,11 +261,12 @@
         top = jnp.max(code.reshape(-1, 8, BLOCK), axis=0)
         top = jnp.max(top, axis=0, keepdims=True)
         peak = jnp.maximum(jnp.log1p(top) * 0.125, 1.0)
-        factor = jnp.where(s < count, 0.125 / peak, 0.0)
+        factor = 0.125 / peak
         for h in range(2):
             rows = jnp.log1p(code[h]) * factor
             swapped = jnp.concatenate([rows[:, 4:], rows[:, :4]], axis=1)
-            out[s, h] = jnp.where(y % 2 == 1 - h, swapped, rows)
+            rows = jnp.where(y % 2 == 1 - h, swapped, rows)
+            out[s, h] = jnp.where(s < count, rows, 0.0)
             half = y // 2 if h == 0 else 1 - y // 2
             copy = pltpu.make_async_copy(out.at[s, h], out_hbm.at[s, :, half], sem.at[s, h])
             copy.start()
@@ -261,6 +290,7 @@
             pltpu.VMEM((BLOCK, 768), jnp.bfloat16),
             pltpu.VMEM((768,), jnp.float32),
             pltpu.VMEM((NB * BLOCK,), jnp.float32),
+            pltpu.VMEM((NB, 1, BLOCK), jnp.float32),
             pltpu.SMEM((1, OWNERS), jnp.int32),
             pltpu.VMEM((SHARD, BLOCK), jnp.bfloat16),
             pltpu.VMEM((SHARD, BLOCK), jnp.bfloat16),
@@ -268,12 +298,17 @@
             pltpu.VMEM((2, SHARD, BLOCK), jnp.bfloat16),
             pltpu.VMEM((2, SHARD, BLOCK), jnp.bfloat16),
             pltpu.VMEM((4, CHUNK, 768), jnp.bfloat16),
-            pltpu.VMEM((STEPS, 768, TILE), jnp.bfloat16),
+            pltpu.VMEM((NB, 768, BLOCK), jnp.bfloat16),
             pltpu.VMEM((2, NB, 8, BLOCK), jnp.float32),
+            pltpu.VMEM((NB, 8, BLOCK), jnp.float32),
             pltpu.VMEM((2, OWNERS, 16, BLOCK), jnp.bfloat16),
             pltpu.SMEM((OWNERS,), jnp.int32),
+            pltpu.SMEM((OWNERS,), jnp.int32),
+            pltpu.VMEM((8, BLOCK), jnp.int32),
+            pltpu.SMEM((8, BLOCK), jnp.int32),
             pltpu.SemaphoreType.DMA((6,)),
-            pltpu.SemaphoreType.DMA((STEPS,)),
+            pltpu.SemaphoreType.DMA,
+            pltpu.SemaphoreType.DMA,
             pltpu.SemaphoreType.DMA((7,)),
             pltpu.SemaphoreType.DMA((7,)),
             pltpu.SemaphoreType.REGULAR((5, 2)),

time: 30.3 us -> 29.8 us (0.983)
  Pallas kernels: 30.2 us -> 29.7 us
    pallas_call x1, Pallas kernels: 28.7 us -> 28.2 us  [shards(): pl.pallas_call(index_kernel, out_shape=jax.ShapeDtypeStruct((2, OWNERS, 1...]
where the time goes in v6:
time: 29.8 us; the launch traced here: 29.7 us
  Pallas kernels  29.7 us (100%)
    pallas_call x1, Pallas kernels, shards(): pl.pallas_call(index_kernel, out_shape=jax.ShapeDtypeStruct((2, OWNERS, 1...  28.2 us
    pallas_call x1, Pallas kernels, shards(): pl.pallas_call(scale_kernel, out_shape=jax.ShapeDtypeStruct((2, OWNERS, 2...  1.51 us

profile of v6, /device:TPU:1, one launch (start us, length us, event | category | flops | bytes accessed | tf_op | source)
XLA Modules:
  0.0 29.7 jit_solution(5014304303850634613)
XLA Ops:
  0.0 0.0 copy-start
  0.0 28.2 %index.1.code_ref = bf16[2,32,16,128]{3,2,1,0:T(8,128)(2,1)S(1)} custom-call(bf16[2,80,128]{2,1,0:T(8,128)(2,1)} %tok_hbm.1, s32[2,80]{1,0:T(2,128)} %mask_hbm.1, bf16[128,768]{1,0:T(8,128)(2,1)} %aw_hbm.1, f32[768]{0:T(1024)} %gain_hbm.1, f32[3840]{0:T(1024)} %bias_hbm.1, s32[1,32]{1,0:T(1,128)} %counts_ref.1, bf16[768,3840]{1,0:T(8,128)(2,1)} %hw_hbm.1), custom_call_target="tpu_custom_call" | custom-call | flops 8000000000 | bytes 7000000 | tf_op jit(solution)/shard_map/index/pallas_call | solution.py:282
  28.2 0.0 copy-done
  28.2 1.5 %scale.1 = f32[2,32,2,8,128]{4,3,2,1,0:T(8,128)} custom-call(s32[1,32]{1,0:T(1,128)S(1)} %copy-done, bf16[2,32,16,128]{3,2,1,0:T(8,128)(2,1)S(1)} %index.1.code_ref), custom_call_target="tpu_custom_call" | custom-call | flops 4000000 | bytes 800000 | tf_op jit(solution)/shard_map/scale/pallas_call | solution.py:332
Async XLA Ops:
  0.0 28.2 %copy-start = (s32[1,32]{1,0:T(1,128)S(1)}, s32[1,32]{1,0:T(1,128)}, u32[]{:S(2)}) copy-start(s32[1,32]{1,0:T(1,128)} %counts_ref.1) | copy-start | bytes 388

commit v7 on v6

--- a/solution.py
+++ b/solution.py
@@ -23,9 +23,9 @@
 
 
 def index_kernel(
-    tok_hbm, mask_hbm, aw_hbm, gain_hbm, bias_hbm, counts_hbm, hw_hbm, recv_ref,
+    tok_hbm, mask_hbm, aw_hbm, gain_hbm, bias_hbm, counts_hbm, hw_hbm, out_ref,
     tok_ref, mask_ref, aw_ref, gain_ref, bias_ref, bias2, counts_ref,
-    tok_own, tok_a, tok_b, tok_c, tok_d, hid, wbuf, pooled, pooled_last, send, starts, firsts, order_v, order,
+    tok_own, tok_a, tok_b, tok_c, tok_d, hid, wbuf, pooled, pooled_last, send, recv_ref, impact, starts, firsts, order_v, order,
     arg_sem, wsem, order_sem, tok_send, tok_recv, ready, tile_send, tile_recv, tile_own,
 ):
     d = lax.axis_index("docs")
@@ -241,49 +241,47 @@
         send_tile(1, r)
     keep_tile(1)
 
+    def tiles_in(k):
+        pltpu.make_async_copy(send.at[k, d], recv_ref.at[k, d], tile_own.at[k]).wait()
+        others = recv_ref.at[k, 0 : OWNERS - 1]
+        pltpu.make_async_copy(others, others, tile_recv.at[k]).wait()
+
+    def codes(k, s):
+        return recv_ref[k, :, s * 8 : (s + 1) * 8, :].astype(jnp.float32)
+
+    def in_order(k, rows):
+        return jnp.where(y % 2 == 1 - k, jnp.concatenate([rows[:, 4:], rows[:, :4]], axis=1), rows)
+
+    tiles_in(0)
+    tops = []
+    for s in range(2):
+        code = codes(0, s)
+        tops.append(jnp.max(code, axis=0))
+        impact[s] = in_order(0, jnp.log1p(code))
     for r in range(7):
         token_copy(r, c).wait_send()
-    for k in range(2):
-        pltpu.make_async_copy(send.at[k, d], recv_ref.at[k, d], tile_own.at[k]).wait()
-        others = send.at[k, 0 : OWNERS - 1]
-        pltpu.make_async_copy(others, others, tile_send.at[k]).wait()
-        others = recv_ref.at[k, 0 : OWNERS - 1]
-        pltpu.make_async_copy(others, others, tile_recv.at[k]).wait()
-
-
-def scale_kernel(counts_ref, code_ref, out_hbm, out, sem):
-    owner = lax.axis_index("docs")
-    y = lax.axis_index("vocab") // 2
-    count = counts_ref[0, owner]
-    copies = []
+    sent = send.at[0, 0 : OWNERS - 1]
+    pltpu.make_async_copy(sent, sent, tile_send.at[0]).wait()
+
+    tiles_in(1)
+    count = jnp.full((8, BLOCK), counts_ref[0, d])
     for s in range(2):
-        code = code_ref[:, :, s * 8 : (s + 1) * 8, :].astype(jnp.float32)
-        top = jnp.max(code.reshape(-1, 8, BLOCK), axis=0)
-        top = jnp.max(top, axis=0, keepdims=True)
-        peak = jnp.maximum(jnp.log1p(top) * 0.125, 1.0)
-        factor = 0.125 / peak
-        for h in range(2):
-            rows = jnp.log1p(code[h]) * factor
-            swapped = jnp.concatenate([rows[:, 4:], rows[:, :4]], axis=1)
-            rows = jnp.where(y % 2 == 1 - h, swapped, rows)
-            out[s, h] = jnp.where(s < count, rows, 0.0)
-            half = y // 2 if h == 0 else 1 - y // 2
-            copy = pltpu.make_async_copy(out.at[s, h], out_hbm.at[s, :, half], sem.at[s, h])
-            copy.start()
-            copies.append(copy)
-    for copy in copies:
-        copy.wait()
+        code = codes(1, s)
+        top = jnp.max(jnp.maximum(tops[s], jnp.max(code, axis=0)), axis=0, keepdims=True)
+        factor = 0.125 / jnp.maximum(jnp.log1p(top) * 0.125, 1.0)
+        out_ref[s, :, y // 2] = jnp.where(count > s, impact[s] * factor, 0.0)
+        out_ref[s, :, 1 - y // 2] = jnp.where(count > s, in_order(1, jnp.log1p(code)) * factor, 0.0)
+    sent = send.at[1, 0 : OWNERS - 1]
+    pltpu.make_async_copy(sent, sent, tile_send.at[1]).wait()
 
 
 def shards(tokens, token_mask, adapter_weight, norm_gain, head_weight, head_bias, block_counts):
-    vmem = pl.BlockSpec(memory_space=pltpu.VMEM)
-    smem = pl.BlockSpec(memory_space=pltpu.SMEM)
     hbm = pl.BlockSpec(memory_space=pltpu.HBM)
-    codes = pl.pallas_call(
+    scaled = pl.pallas_call(
         index_kernel,
-        out_shape=jax.ShapeDtypeStruct((2, OWNERS, 16, BLOCK), jnp.bfloat16),
+        out_shape=jax.ShapeDtypeStruct((2, OWNERS, 2, 8, BLOCK), jnp.float32),
         in_specs=[hbm] * 7,
-        out_specs=pl.BlockSpec(memory_space=pl.ANY),
+        out_specs=pl.BlockSpec(memory_space=pltpu.VMEM),
         scratch_shapes=[
             pltpu.VMEM((2, LEN, BLOCK), jnp.bfloat16),
             pltpu.VMEM((2, LEN), jnp.int32),
@@ -302,6 +300,8 @@
             pltpu.VMEM((2, NB, 8, BLOCK), jnp.float32),
             pltpu.VMEM((NB, 8, BLOCK), jnp.float32),
             pltpu.VMEM((2, OWNERS, 16, BLOCK), jnp.bfloat16),
+            pltpu.VMEM((2, OWNERS, 16, BLOCK), jnp.bfloat16),
+            pltpu.VMEM((2, OWNERS, 8, BLOCK), jnp.float32),
             pltpu.SMEM((OWNERS,), jnp.int32),
             pltpu.SMEM((OWNERS,), jnp.int32),
             pltpu.VMEM((8, BLOCK), jnp.int32),
@@ -329,19 +329,6 @@
             tokens, token_mask, adapter_weight, norm_gain, head_bias, block_counts, head_weight
         )
     ))
-    scaled = pl.pallas_call(
-        scale_kernel,
-        out_shape=jax.ShapeDtypeStruct((2, OWNERS, 2, 8, BLOCK), jnp.float32),
-        in_specs=[smem, vmem],
-        out_specs=hbm,
-        scratch_shapes=[
-            pltpu.VMEM((2, 2, OWNERS, 8, BLOCK), jnp.float32),
-            pltpu.SemaphoreType.DMA((2, 2)),
-        ],
-        compiler_params=pltpu.CompilerParams(vmem_limit_bytes=8 * 2**20),
-        cost_estimate=pl.CostEstimate(flops=4_000_000, bytes_accessed=800_000, transcendentals=131072),
-        name="scale",
-    )(block_counts, codes)
     return scaled.reshape(2, OWNERS * 16, BLOCK)
 
 

time: 29.8 us -> 29.2 us (0.980)
  Pallas kernels: 29.7 us -> 28.3 us
  local copies, waits for them, and re-layouts: 0.01 us -> 0.8 us
    pallas_call x2 -> x1, Pallas kernels: 29.7 us -> 28.3 us  [shards(): pl.pallas_call(index_kernel, out_shape=jax.ShapeDtypeStruct((2, OWNERS, 2...]
    unnamed x2 -> x1, local copies, waits for them, and re-layouts: 0.01 us -> 0.8 us
where the time goes in v7:
time: 29.2 us; the launch traced here: 29.1 us
  Pallas kernels  28.3 us (97%)
  local copies, waits for them, and re-layouts  0.8 us (3%)
    pallas_call x1, Pallas kernels, shards(): pl.pallas_call(index_kernel, out_shape=jax.ShapeDtypeStruct((2, OWNERS, 2...  28.3 us
    unnamed x1, local copies, waits for them, and re-layouts  0.8 us

profile of v7, /device:TPU:1, one launch (start us, length us, event | category | flops | bytes accessed | tf_op | source)
XLA Modules:
  0.0 29.1 jit_solution(16155128879379831654)
XLA Ops:
  0.0 28.3 %index.1 = f32[2,32,2,8,128]{4,3,2,1,0:T(8,128)S(1)} custom-call(bf16[2,80,128]{2,1,0:T(8,128)(2,1)} %tok_hbm.1, s32[2,80]{1,0:T(2,128)} %mask_hbm.1, bf16[128,768]{1,0:T(8,128)(2,1)} %aw_hbm.1, f32[768]{0:T(1024)} %gain_hbm.1, f32[3840]{0:T(1024)} %bias_hbm.1, s32[1,32]{1,0:T(1,128)} %counts_hbm.1, bf16[768,3840]{1,0:T(8,128)(2,1)} %hw_hbm.1), custom_call_target="tpu_custom_call" | custom-call | flops 8000000000 | bytes 7000000 | tf_op jit(solution)/shard_map/index/pallas_call | solution.py:280
  28.3 0.8 %copy.9 = f32[2,512,128]{2,1,0:T(8,128)} copy(f32[2,512,128]{2,1,0:T(8,128)S(1)} %bitcast.1) | data formatting | bytes 1048576

commit v8 on v7

--- a/solution.py
+++ b/solution.py
@@ -25,7 +25,7 @@
 def index_kernel(
     tok_hbm, mask_hbm, aw_hbm, gain_hbm, bias_hbm, counts_hbm, hw_hbm, out_ref,
     tok_ref, mask_ref, aw_ref, gain_ref, bias_ref, bias2, counts_ref,
-    tok_own, tok_a, tok_b, tok_c, tok_d, hid, wbuf, pooled, pooled_last, send, recv_ref, impact, starts, firsts, order_v, order,
+    tok_own, tok_a, tok_b0, tok_b1, tok_c, tok_d, hid, wbuf, pooled, pooled_last, send, recv_ref, impact, starts, firsts, order_v, order,
     arg_sem, wsem, order_sem, tok_send, tok_recv, ready, tile_send, tile_recv, tile_own,
 ):
     d = lax.axis_index("docs")
@@ -72,12 +72,12 @@
 
     pl.semaphore_wait(barrier, 11)
 
-    buffers = [None, tok_b, tok_b, tok_c, tok_c, tok_d, tok_d]
+    buffers = [tok_a, tok_b0, tok_b1, tok_c, tok_c, tok_d, tok_d]
 
     def token_copy(r, core):
         return pltpu.make_async_remote_copy(
             src_ref=tok_own,
-            dst_ref=tok_a if r == 0 else buffers[r].at[core],
+            dst_ref=buffers[r] if r < 3 else buffers[r].at[core],
             send_sem=tok_send.at[r],
             recv_sem=tok_recv.at[r],
             device_id=(d, partners[r]),
@@ -203,13 +203,17 @@
     for i in range(STEPS - 1):
         head_step(0, i)
 
-    tokens_in(1)
-    tokens_in(2)
+    def norm_near(buf, core):
+        for i in range(2):
+            norm_rows(buf[i * LEN : (i + 1) * LEN], 1, pl.multiple_of(core * SHARD + i * LEN, 16))
+
     told(1)
     tell(2)
+    tokens_in(1)
     head_step(0, STEPS - 1)
-    for i in range(4):
-        norm_chunk(1, tok_b, i, 4)
+    norm_near(tok_b0, c)
+    tokens_in(2)
+    norm_near(tok_b1, 1 - c)
     tokens_in(3)
     tokens_in(4)
     told(2)
@@ -235,9 +239,10 @@
     early = TILE // BLOCK // 2
     for i in range(STEPS):
         head_step(3, i)
-        for r in range(i * early, min((i + 1) * early, OWNERS - 1)):
-            send_tile(1, r)
-    for r in range(STEPS * early, OWNERS - 1):
+        if i % 2:
+            for r in range((i - 1) * early, min((i + 1) * early, OWNERS - 1)):
+                send_tile(1, r)
+    for r in range((STEPS - 1) * early, OWNERS - 1):
         send_tile(1, r)
     keep_tile(1)
 
@@ -292,7 +297,8 @@
             pltpu.SMEM((1, OWNERS), jnp.int32),
             pltpu.VMEM((SHARD, BLOCK), jnp.bfloat16),
             pltpu.VMEM((SHARD, BLOCK), jnp.bfloat16),
-            pltpu.VMEM((2, SHARD, BLOCK), jnp.bfloat16),
+            pltpu.VMEM((SHARD, BLOCK), jnp.bfloat16),
+            pltpu.VMEM((SHARD, BLOCK), jnp.bfloat16),
             pltpu.VMEM((2, SHARD, BLOCK), jnp.bfloat16),
             pltpu.VMEM((2, SHARD, BLOCK), jnp.bfloat16),
             pltpu.VMEM((4, CHUNK, 768), jnp.bfloat16),

time: 29.2 us -> 28.6 us (0.979)
  Pallas kernels: 28.3 us -> 27.8 us
    pallas_call x1, Pallas kernels: 28.3 us -> 27.8 us  [shards(): pl.pallas_call(index_kernel, out_shape=jax.ShapeDtypeStruct((2, OWNERS, 2...]
where the time goes in v8:
time: 28.6 us
  Pallas kernels  27.8 us (97%)
  local copies, waits for them, and re-layouts  0.8 us (3%)
    pallas_call x1, Pallas kernels, shards(): pl.pallas_call(index_kernel, out_shape=jax.ShapeDtypeStruct((2, OWNERS, 2...  27.8 us
    unnamed x1, local copies, waits for them, and re-layouts  0.8 us

profile of v8, /device:TPU:1, one launch (start us, length us, event | category | flops | bytes accessed | tf_op | source)
XLA Modules:
  0.0 28.6 jit_solution(2364601266518961252)
XLA Ops:
  0.0 27.8 %index.1 = f32[2,32,2,8,128]{4,3,2,1,0:T(8,128)S(1)} custom-call(bf16[2,80,128]{2,1,0:T(8,128)(2,1)} %tok_hbm.1, s32[2,80]{1,0:T(2,128)} %mask_hbm.1, bf16[128,768]{1,0:T(8,128)(2,1)} %aw_hbm.1, f32[768]{0:T(1024)} %gain_hbm.1, f32[3840]{0:T(1024)} %bias_hbm.1, s32[1,32]{1,0:T(1,128)} %counts_hbm.1, bf16[768,3840]{1,0:T(8,128)(2,1)} %hw_hbm.1), custom_call_target="tpu_custom_call" | custom-call | flops 8000000000 | bytes 7000000 | tf_op jit(solution)/shard_map/index/pallas_call | solution.py:285
  27.8 0.8 %copy.9 = f32[2,512,128]{2,1,0:T(8,128)} copy(f32[2,512,128]{2,1,0:T(8,128)S(1)} %bitcast.1) | data formatting | bytes 1048576

commit v9 on v8

--- a/solution.py
+++ b/solution.py
@@ -239,10 +239,10 @@
     early = TILE // BLOCK // 2
     for i in range(STEPS):
         head_step(3, i)
-        if i % 2:
-            for r in range((i - 1) * early, min((i + 1) * early, OWNERS - 1)):
+        if i == 2:
+            for r in range(min(3 * early, OWNERS - 1)):
                 send_tile(1, r)
-    for r in range((STEPS - 1) * early, OWNERS - 1):
+    for r in range(3 * early, OWNERS - 1):
         send_tile(1, r)
     keep_tile(1)
 

time: 28.6 us -> 28.7 us (level)
  no operation moved by 1% of the time
where the time goes in v9:
time: 28.7 us; the launch traced here: 28.6 us
  Pallas kernels  27.8 us (97%)
  local copies, waits for them, and re-layouts  0.8 us (3%)
    pallas_call x1, Pallas kernels, shards(): pl.pallas_call(index_kernel, out_shape=jax.ShapeDtypeStruct((2, OWNERS, 2...  27.8 us
    unnamed x1, local copies, waits for them, and re-layouts  0.8 us

profile of v9, /device:TPU:1, one launch (start us, length us, event | category | flops | bytes accessed | tf_op | source)
XLA Modules:
  0.0 28.6 jit_solution(120762390921830862)
XLA Ops:
  0.0 27.8 %index.1 = f32[2,32,2,8,128]{4,3,2,1,0:T(8,128)S(1)} custom-call(bf16[2,80,128]{2,1,0:T(8,128)(2,1)} %tok_hbm.1, s32[2,80]{1,0:T(2,128)} %mask_hbm.1, bf16[128,768]{1,0:T(8,128)(2,1)} %aw_hbm.1, f32[768]{0:T(1024)} %gain_hbm.1, f32[3840]{0:T(1024)} %bias_hbm.1, s32[1,32]{1,0:T(1,128)} %counts_hbm.1, bf16[768,3840]{1,0:T(8,128)(2,1)} %hw_hbm.1), custom_call_target="tpu_custom_call" | custom-call | flops 8000000000 | bytes 7000000 | tf_op jit(solution)/shard_map/index/pallas_call | solution.py:285
  27.8 0.8 %copy.9 = f32[2,512,128]{2,1,0:T(8,128)} copy(f32[2,512,128]{2,1,0:T(8,128)S(1)} %bitcast.1) | data formatting | bytes 1048576
